TPU v7x, 32 devices: a whole 2x2x4 slice. The times are simulated.
32 devices in a mesh: seq: 2 (over x), fsdp: 16 (over z, y, core).
Axes of the slice: x: 2, y: 2, z: 4, core: 2. Of those that a mesh axis runs over, the one named last changes fastest.
Arguments:
- block_input: float32 [16, 512, 1024], P('fsdp', 'seq'), may hold values from -6 to 6
- key_mask: int32 [16, 512], P('fsdp'), may hold values from 0 to 1, as said below
- first_gain: bfloat16 [1024], P('fsdp'), may hold values from 0.5 to 1.5
- first_shift: bfloat16 [1024], P('fsdp'), may hold values from -3 to 3
- qkv_weight: bfloat16 [1024, 3072], P('fsdp'), may hold values from -0.1875 to 0.1875
- query_bias: bfloat16 [1024], P('fsdp'), may hold values from -3 to 3
- value_bias: bfloat16 [1024], P('fsdp'), may hold values from -3 to 3
- proj_weight: bfloat16 [1024, 1024], P('fsdp'), may hold values from -1.5 to 1.5
- proj_bias: bfloat16 [1024], P('fsdp'), may hold values from -3 to 3
- first_scale: bfloat16 [1024], P('fsdp'), may hold values from 0.5 to 2
- second_gain: bfloat16 [1024], P('fsdp'), may hold values from 0.5 to 1.5
- second_shift: bfloat16 [1024], P('fsdp'), may hold values from -3 to 3
- fc1_weight: bfloat16 [1024, 4096], P('fsdp'), may hold values from -0.1875 to 0.1875
- fc1_bias: bfloat16 [4096], P('fsdp'), may hold values from -3 to 3
- fc2_weight: bfloat16 [4096, 1024], P('fsdp'), may hold values from -0.09375 to 0.09375
- fc2_bias: bfloat16 [1024], P('fsdp'), may hold values from -3 to 3
- second_scale: bfloat16 [1024], P('fsdp'), may hold values from 0.5 to 2
- cotangent: float32 [16, 512, 1024], P('fsdp', 'seq'), may hold values from -6 to 6
Outputs:
- block_output: float32 [16, 512, 1024], P('fsdp', 'seq')
- input_grad: float32 [16, 512, 1024], P('fsdp', 'seq')
- first_gain_grad: float32 [1024], P('fsdp')
- first_shift_grad: float32 [1024], P('fsdp')
- qkv_weight_grad: float32 [1024, 3072], P('fsdp')
- query_bias_grad: float32 [1024], P('fsdp')
- value_bias_grad: float32 [1024], P('fsdp')
- proj_weight_grad: float32 [1024, 1024], P('fsdp')
- proj_bias_grad: float32 [1024], P('fsdp')
- first_scale_grad: float32 [1024], P('fsdp')
- second_gain_grad: float32 [1024], P('fsdp')
- second_shift_grad: float32 [1024], P('fsdp')
- fc1_weight_grad: float32 [1024, 4096], P('fsdp')
- fc1_bias_grad: float32 [4096], P('fsdp')
- fc2_weight_grad: float32 [4096, 1024], P('fsdp')
- fc2_bias_grad: float32 [1024], P('fsdp')
- second_scale_grad: float32 [1024], P('fsdp')
Inputs may be any that keep to these rules, and one draw needn't show every extreme that they name: `key_mask`: each row is ones on a leading run of positions and zeros after it; its first position is 1 and its last is 0.
All inputs are finite; a program needn't handle non-finite values.
Results may differ from a plain program's by a relative error of at most 0.012.
The roundings to bfloat16 on the way count: a program that leaves them out, or rounds other values in their place, can miss the bound.
Values may be sent and summed in bfloat16 or wider, within the bound.
A program may use at most 192 MiB of HBM per device.

v0:
```python
import jax
import jax.numpy as jnp
from jax import lax
from jax.sharding import PartitionSpec as P

HEADS = 16
HD = 64


EPSILON = 1e-06
ROOT_HALF = 0.7071067811865476
INV_ROOT_TAU = 0.3989422804014327


def normalize(values, gain, shift):
    centre = values - jnp.mean(values, axis=-1, keepdims=True)
    spread_inv = lax.rsqrt(jnp.mean(centre * centre, axis=-1, keepdims=True) + EPSILON)
    unit = centre * spread_inv
    return (unit * gain + shift, unit, spread_inv)


def normalize_back(grad_out, unit, spread_inv, gain):
    scaled = grad_out * gain
    return spread_inv * (
        scaled
        - jnp.mean(scaled, axis=-1, keepdims=True)
        - unit * jnp.mean(scaled * unit, axis=-1, keepdims=True)
    )


def smooth_gate(values):
    return 0.5 * values * (1.0 + lax.erf(values * ROOT_HALF))


def gate_slope(values):
    return (
        0.5 * (1.0 + lax.erf(values * ROOT_HALF))
        + values * jnp.exp(-0.5 * values * values) * INV_ROOT_TAU
    )


def wide(values):
    return values.astype(jnp.float32)


def score_table(query, keys, valid):
    factor = query.shape[-1] ** (-0.5)
    scores = jnp.einsum("qhd,khd->hqk", query, keys, preferred_element_type=jnp.float32) * factor
    return jnp.where(valid[None, None, :], scores, -jnp.inf)


def attend(query, keys, values, valid):
    scores = score_table(query, keys, valid)
    row_top = jnp.max(scores, axis=-1, keepdims=True)
    log_total = row_top + jnp.log(jnp.sum(jnp.exp(scores - row_top), axis=-1, keepdims=True))
    weights = jnp.exp(scores - log_total).astype(jnp.bfloat16)
    attended = jnp.einsum(
        "hqk,khd->qhd", weights, values, preferred_element_type=jnp.float32
    ).astype(jnp.bfloat16)
    return (attended, log_total)


def attend_back(query, keys, values, attended, log_total, grad_attended, valid):
    factor = query.shape[-1] ** (-0.5)
    scores = score_table(query, keys, valid)
    prob = jnp.exp(scores - log_total)
    weights = prob.astype(jnp.bfloat16)
    grad_values = jnp.einsum(
        "hqk,qhd->khd", weights, grad_attended, preferred_element_type=jnp.float32
    ).astype(jnp.bfloat16)
    grad_prob = jnp.einsum(
        "qhd,khd->hqk", grad_attended, values, preferred_element_type=jnp.float32
    )
    delta = jnp.einsum("qhd,qhd->hq", grad_attended, attended, preferred_element_type=jnp.float32)[
        :, :, None
    ]
    grad_scores = (prob * (grad_prob - delta) * factor).astype(jnp.bfloat16)
    grad_query = jnp.einsum(
        "hqk,khd->qhd", grad_scores, keys, preferred_element_type=jnp.float32
    ).astype(jnp.bfloat16)
    grad_keys = jnp.einsum(
        "hqk,qhd->khd", grad_scores, query, preferred_element_type=jnp.float32
    ).astype(jnp.bfloat16)
    return (grad_query, grad_keys, grad_values)


def on_device(
    block_input,
    key_mask,
    first_gain,
    first_shift,
    qkv_weight,
    query_bias,
    value_bias,
    proj_weight,
    proj_bias,
    first_scale,
    second_gain,
    second_shift,
    fc1_weight,
    fc1_bias,
    fc2_weight,
    fc2_bias,
    second_scale,
    cotangent,
):
    gathered = (
        lax.all_gather(first_gain, "fsdp", axis=0, tiled=True),
        lax.all_gather(first_shift, "fsdp", axis=0, tiled=True),
        lax.all_gather(qkv_weight, "fsdp", axis=0, tiled=True),
        lax.all_gather(query_bias, "fsdp", axis=0, tiled=True),
        lax.all_gather(value_bias, "fsdp", axis=0, tiled=True),
        lax.all_gather(proj_weight, "fsdp", axis=0, tiled=True),
        lax.all_gather(proj_bias, "fsdp", axis=0, tiled=True),
        lax.all_gather(first_scale, "fsdp", axis=0, tiled=True),
        lax.all_gather(second_gain, "fsdp", axis=0, tiled=True),
        lax.all_gather(second_shift, "fsdp", axis=0, tiled=True),
        lax.all_gather(fc1_weight, "fsdp", axis=0, tiled=True),
        lax.all_gather(fc1_bias, "fsdp", axis=0, tiled=True),
        lax.all_gather(fc2_weight, "fsdp", axis=0, tiled=True),
        lax.all_gather(fc2_bias, "fsdp", axis=0, tiled=True),
        lax.all_gather(second_scale, "fsdp", axis=0, tiled=True),
    )
    (
        gain_one,
        shift_one,
        joint_full,
        qbias_full,
        vbias_full,
        proj_full,
        pbias_full,
        scale_one,
        gain_two,
        shift_two,
        expand_full,
        ebias_full,
        reduce_full,
        rbias_full,
        scale_two,
    ) = gathered
    width = joint_full.shape[0]
    tokens = block_input[0]
    count = tokens.shape[0]
    valid = key_mask[0] > 0
    length = valid.shape[0]
    seq_count = lax.axis_size("seq")
    heads_here = HEADS // seq_count
    local_cols = heads_here * HD
    normed1, unit1, inv1 = normalize(tokens, wide(gain_one), wide(shift_one))
    act1 = normed1.astype(jnp.bfloat16)
    joint_bias = jnp.concatenate(
        [wide(qbias_full), jnp.zeros((width,), jnp.float32), wide(vbias_full)]
    )
    joint = (jnp.dot(act1, joint_full, preferred_element_type=jnp.float32) + joint_bias).astype(
        jnp.bfloat16
    )
    spread = lax.all_to_all(
        joint.reshape(count, 3, seq_count, local_cols),
        "seq",
        split_axis=2,
        concat_axis=0,
        tiled=True,
    )
    spread = spread.reshape(length, 3, heads_here, HD)
    query = spread[:, 0]
    keys = spread[:, 1]
    values = spread[:, 2]
    attended, log_total = attend(query, keys, values, valid)
    returned = lax.all_to_all(
        attended.reshape(length, 1, local_cols), "seq", split_axis=0, concat_axis=1, tiled=True
    )
    attended_flat = returned.reshape(count, width)
    mixed = jnp.dot(attended_flat, proj_full, preferred_element_type=jnp.float32) + wide(pbias_full)
    resid = tokens + wide(scale_one) * mixed
    normed2, unit2, inv2 = normalize(resid, wide(gain_two), wide(shift_two))
    act2 = normed2.astype(jnp.bfloat16)
    pre = jnp.dot(act2, expand_full, preferred_element_type=jnp.float32) + wide(ebias_full)
    hidden = smooth_gate(pre).astype(jnp.bfloat16)
    branch = jnp.dot(hidden, reduce_full, preferred_element_type=jnp.float32) + wide(rbias_full)
    result = resid + wide(scale_two) * branch
    again = (
        lax.all_gather(qkv_weight, "fsdp", axis=0, tiled=True),
        lax.all_gather(proj_weight, "fsdp", axis=0, tiled=True),
        lax.all_gather(first_gain, "fsdp", axis=0, tiled=True),
        lax.all_gather(first_scale, "fsdp", axis=0, tiled=True),
        lax.all_gather(second_gain, "fsdp", axis=0, tiled=True),
        lax.all_gather(second_scale, "fsdp", axis=0, tiled=True),
        lax.all_gather(fc1_weight, "fsdp", axis=0, tiled=True),
        lax.all_gather(fc2_weight, "fsdp", axis=0, tiled=True),
    )
    (
        back_joint,
        back_proj,
        back_gain1,
        back_scale1,
        back_gain2,
        back_scale2,
        back_expand,
        back_reduce,
    ) = again
    grad_out = cotangent[0]
    grad_scale2 = jnp.sum(grad_out * branch, axis=0)
    grad_branch = wide(back_scale2) * grad_out
    grad_bias2 = jnp.sum(grad_branch, axis=0)
    branch_low = grad_branch.astype(jnp.bfloat16)
    grad_reduce = jnp.einsum("tf,td->fd", hidden, branch_low, preferred_element_type=jnp.float32)
    grad_hidden = jnp.einsum(
        "td,fd->tf", branch_low, back_reduce, preferred_element_type=jnp.float32
    )
    grad_pre = grad_hidden * gate_slope(pre)
    grad_bias1 = jnp.sum(grad_pre, axis=0)
    pre_low = grad_pre.astype(jnp.bfloat16)
    grad_expand = jnp.einsum("td,tf->df", act2, pre_low, preferred_element_type=jnp.float32)
    grad_act2 = jnp.einsum("tf,df->td", pre_low, back_expand, preferred_element_type=jnp.float32)
    grad_gain2 = jnp.sum(grad_act2 * unit2, axis=0)
    grad_shift2 = jnp.sum(grad_act2, axis=0)
    grad_resid = grad_out + normalize_back(grad_act2, unit2, inv2, wide(back_gain2))
    grad_scale1 = jnp.sum(grad_resid * mixed, axis=0)
    grad_mixed = wide(back_scale1) * grad_resid
    grad_pbias = jnp.sum(grad_mixed, axis=0)
    mixed_low = grad_mixed.astype(jnp.bfloat16)
    grad_proj = jnp.einsum(
        "td,te->de", attended_flat, mixed_low, preferred_element_type=jnp.float32
    )
    grad_attended = jnp.einsum(
        "te,de->td", mixed_low, back_proj, preferred_element_type=jnp.float32
    ).astype(jnp.bfloat16)
    grad_spread = lax.all_to_all(
        grad_attended.reshape(count, seq_count, local_cols),
        "seq",
        split_axis=1,
        concat_axis=0,
        tiled=True,
    )
    grad_heads = grad_spread.reshape(length, heads_here, HD)
    grad_query, grad_keys, grad_values = attend_back(
        query, keys, values, attended, log_total, grad_heads, valid
    )
    stacked = jnp.stack((grad_query, grad_keys, grad_values), axis=1).reshape(
        length, 3, 1, local_cols
    )
    grad_back = lax.all_to_all(stacked, "seq", split_axis=0, concat_axis=2, tiled=True)
    grad_joint = grad_back.reshape(count, 3 * width)
    grad_qbias = jnp.sum(wide(grad_joint[:, :width]), axis=0)
    grad_vbias = jnp.sum(wide(grad_joint[:, 2 * width :]), axis=0)
    grad_qkv = jnp.einsum("td,te->de", act1, grad_joint, preferred_element_type=jnp.float32)
    grad_act1 = jnp.einsum("te,de->td", grad_joint, back_joint, preferred_element_type=jnp.float32)
    grad_gain1 = jnp.sum(grad_act1 * unit1, axis=0)
    grad_shift1 = jnp.sum(grad_act1, axis=0)
    grad_in = grad_resid + normalize_back(grad_act1, unit1, inv1, wide(back_gain1))
    owned = (
        lax.psum_scatter(grad_gain1, "fsdp", scatter_dimension=0, tiled=True),
        lax.psum_scatter(grad_shift1, "fsdp", scatter_dimension=0, tiled=True),
        lax.psum_scatter(grad_qkv, "fsdp", scatter_dimension=0, tiled=True),
        lax.psum_scatter(grad_qbias, "fsdp", scatter_dimension=0, tiled=True),
        lax.psum_scatter(grad_vbias, "fsdp", scatter_dimension=0, tiled=True),
        lax.psum_scatter(grad_proj, "fsdp", scatter_dimension=0, tiled=True),
        lax.psum_scatter(grad_pbias, "fsdp", scatter_dimension=0, tiled=True),
        lax.psum_scatter(grad_scale1, "fsdp", scatter_dimension=0, tiled=True),
        lax.psum_scatter(grad_gain2, "fsdp", scatter_dimension=0, tiled=True),
        lax.psum_scatter(grad_shift2, "fsdp", scatter_dimension=0, tiled=True),
        lax.psum_scatter(grad_expand, "fsdp", scatter_dimension=0, tiled=True),
        lax.psum_scatter(grad_bias1, "fsdp", scatter_dimension=0, tiled=True),
        lax.psum_scatter(grad_reduce, "fsdp", scatter_dimension=0, tiled=True),
        lax.psum_scatter(grad_bias2, "fsdp", scatter_dimension=0, tiled=True),
        lax.psum_scatter(grad_scale2, "fsdp", scatter_dimension=0, tiled=True),
    )
    (
        own_g1,
        own_s1,
        own_qkv,
        own_qb,
        own_vb,
        own_proj,
        own_pb,
        own_l1,
        own_g2,
        own_s2,
        own_fc1,
        own_b1,
        own_fc2,
        own_b2,
        own_l2,
    ) = owned
    summed = lax.psum(
        (
            own_g1,
            own_s1,
            own_qkv,
            own_qb,
            own_vb,
            own_proj,
            own_pb,
            own_l1,
            own_g2,
            own_s2,
            own_fc1,
            own_b1,
            own_fc2,
            own_b2,
            own_l2,
        ),
        "seq",
    )
    return (
        result[None],
        grad_in[None],
        summed[0],
        summed[1],
        summed[2],
        summed[3],
        summed[4],
        summed[5],
        summed[6],
        summed[7],
        summed[8],
        summed[9],
        summed[10],
        summed[11],
        summed[12],
        summed[13],
        summed[14],
    )


def solution(mesh):
    return jax.shard_map(
        on_device,
        mesh=mesh,
        in_specs=(
            P("fsdp", "seq", None),
            P("fsdp", None),
            P("fsdp"),
            P("fsdp"),
            P("fsdp", None),
            P("fsdp"),
            P("fsdp"),
            P("fsdp", None),
            P("fsdp"),
            P("fsdp"),
            P("fsdp"),
            P("fsdp"),
            P("fsdp", None),
            P("fsdp"),
            P("fsdp", None),
            P("fsdp"),
            P("fsdp"),
            P("fsdp", "seq", None),
        ),
        out_specs=(
            P("fsdp", "seq", None),
            P("fsdp", "seq", None),
            P("fsdp"),
            P("fsdp"),
            P("fsdp", None),
            P("fsdp"),
            P("fsdp"),
            P("fsdp", None),
            P("fsdp"),
            P("fsdp"),
            P("fsdp"),
            P("fsdp"),
            P("fsdp", None),
            P("fsdp"),
            P("fsdp", None),
            P("fsdp"),
            P("fsdp"),
        ),
        check_vma=False,
    )
```

profile of v0, /device:TPU:0, one launch (start us, length us, event | category | flops | bytes accessed | tf_op | source)
XLA Modules:
  0.0 974.3 jit_solution(12532771214133890240)
XLA Ops:
  20.3 64.0 %all-reduce.24 = (bf16[1024]{0:T(1024)(128)(2,1)S(1)}, bf16[1024]{0:T(1024)(128)(2,1)S(1)}, bf16[1024]{0:T(1024)(128)(2,1)S(1)}, bf16[1024]{0:T(1024)(128)(2,1)S...) all-reduce(bf16[1024]{0:T(1024)(128)(2,1)S(1)} %dynamic-update-slic, ...), channel_id=1, replica_groups=mesh['seq'=2,'fsdp'=16] {'fsdp'}, use_global_device_ids=true, to_apply=%add.4 | all-reduce | flops 10240 | bytes 40960
  87.3 6.2 fusion.6
  102.9 15.2 %all-to-all-done = bf16[256,3,2,512]{3,0,1,2:T(8,128)(2,1)S(1)} async-done(((bf16[256,3,2,512]{3,0,1,2:T(8,128)(2,1)}), bf16[256,3,2,512]{3,0,1,2:T(8,128)(2,1)S(1)}, u32[]{:S(2)}, u32[]{:S(2)}) %all-to-all-start) | async-done | bytes 1572896 | tf_op jit(solution)/shard_map/all_to_all | solution.py:157
  144.3 17.9 %all-gather = bf16[16,1,256]{2,1,0:T(2,128)(2,1)S(1)} all-gather(bf16[1,1,256]{2,1,0:T(2,128)(2,1)S(1)} %reshape.195), channel_id=1, replica_groups=mesh['seq'=2,'fsdp'=16] {'fsdp'}, dimensions={0}, use_global_device_ids=true | all-gather | bytes 8704 | tf_op jit(solution)/shard_map/all_gather | solution.py:119
  172.5 21.2 %all-gather.10.cloned.1.call-done = bf16[1024,4096]{1,0:T(8,128)(2,1)} async-done(((bf16[64,4096]{1,0:T(8,128)(2,1)}), bf16[1024,4096]{1,0:T(8,128)(2,1)}) %all-gather.10.cloned.1.call-update) | async-done | bytes 8388624 | tf_op jit(solution)/shard_map/all_gather | solution.py:118
  193.7 8.1 convolution_add_fusion
  201.8 67.1 %all-gather.12.cloned.1.call-done = bf16[4096,1024]{1,0:T(8,128)(2,1)} async-done(((bf16[256,1024]{1,0:T(8,128)(2,1)}), bf16[4096,1024]{1,0:T(8,128)(2,1)}) %all-gather.12.cloned.1.call-update) | async-done | bytes 8388624 | tf_op jit(solution)/shard_map/all_gather | solution.py:120
  268.9 6.9 fusion.34
  275.8 6.9 multiply_reduce_fusion
  294.3 11.3 %all_to_all.60 = bf16[256,2,512]{2,0,1:T(8,128)(2,1)S(1)} all-to-all(bf16[256,2,512]{2,0,1:T(8,128)(2,1)S(1)} %bitcast.129), channel_id=1, replica_groups=mesh['seq'=2,'fsdp'=16] {'seq'}, dimensions={1} | all-to-all | bytes 1048576 | tf_op jit(solution)/shard_map/all_to_all | solution.py:228
  309.0 4.6 convolution_convert_fusion
  318.4 6.3 multiply_convert_fusion
  334.0 4.9 pad_maximum_fusion
  338.9 27.3 %all_to_all.61 = bf16[512,3,1,512]{3,1,2,0:T(4,128)(2,1)S(1)} all-to-all(bf16[512,3,1,512]{3,1,2,0:T(4,128)(2,1)S(1)} %pad_maximum_fusion), channel_id=1, replica_groups=mesh['seq'=2,'fsdp'=16] {'seq'}, dimensions={0} | all-to-all | bytes 3145728 | tf_op jit(solution)/shard_map/all_to_all | solution.py:242
  369.4 6.5 fusion.17
  376.0 12.7 %fusion.9 = f32[1024,4096]{1,0:T(8,128)} fusion(bf16[256,4096]{1,0:T(8,128)(2,1)} %copy-done.10, f32[256,1024]{1,0:T(8,128)} %copy-done.4, f32[1024]{0:T(1024)S(1)} %convert_element_type.116, f32[1024]{0:T(1024)S(1)} %convert_element_type.115, f32[256]{0:T(256)S(1)} %add_rsqrt_fusion, f32[256]{0:T(256)S(1)} %broadcast_multiply_fusion.4), kind=kOutput, calls=%fused_computation.42 | convolution fusion | flops 2148794368 | bytes 19933184 | tf_op jit(solution)/shard_map/td,tf->df/dot_general | solution.py:213
  389.0 12.1 %fusion.29 = f32[4096,1024]{1,0:T(8,128)} fusion(f32[1,256,1024]{2,1,0:T(8,128)} %param.35, f32[1024]{0:T(1024)S(1)} %convert_element_type.114, f32[256,4096]{1,0:T(8,128)} %convolution_add_fusion), kind=kOutput, calls=%fused_computation.75 | convolution fusion | flops 2153250816 | bytes 22024192 | tf_op jit(solution)/shard_map/tf,td->fd/dot_general | solution.py:206
  401.3 106.4 %reduce-scatter.5.cloned.1.call-done = f32[64,3072]{1,0:T(8,128)} async-done(((f32[1024,3072]{1,0:T(8,128)}), f32[64,3072]{1,0:T(8,128)}) %reduce-scatter.5.cloned.1.call-update) | async-done | bytes 786448 | tf_op jit(solution)/shard_map/reduce_scatter | solution.py:254
  507.7 182.4 %reduce-scatter.9.cloned.1.call-done = f32[64,4096]{1,0:T(8,128)} async-done(((f32[1024,4096]{1,0:T(8,128)}), f32[64,4096]{1,0:T(8,128)}) %reduce-scatter.9.cloned.1.call-update) | async-done | bytes 1048592 | tf_op jit(solution)/shard_map/reduce_scatter | solution.py:262
  690.1 182.2 %reduce-scatter.11.cloned.1.call-done = f32[256,1024]{1,0:T(8,128)} async-done(((f32[4096,1024]{1,0:T(8,128)}), f32[256,1024]{1,0:T(8,128)}) %reduce-scatter.11.cloned.1.call-update) | async-done | bytes 1048592 | tf_op jit(solution)/shard_map/reduce_scatter | solution.py:264
  873.9 5.8 multiply_reduce_fusion.2
  879.7 59.7 %all-reduce.21 = (f32[1024]{0:T(1024)S(1)}, f32[1024]{0:T(1024)S(1)}, f32[1024]{0:T(1024)S(1)}, f32[1024]{0:T(1024)S(1)}, f32[1024]{0:T(1024)S(1)}, /*index=5*/f...) all-reduce(f32[1024]{0:T(1024)S(1)} %get-tuple-element.19, ...), channel_id=2, replica_groups=mesh['seq'=2,'fsdp'=16] {'fsdp'}, use_global_device_ids=true, to_apply=%region_11.12.clone | all-reduce | flops 14336 | bytes 114688
  940.2 5.7 all-reduce.22
  948.8 11.7 %all-reduce.27.cloned.1.call-done = (f32[64,3072]{1,0:T(8,128)}, f32[64,1024]{1,0:T(8,128)}, f32[64,4096]{1,0:T(8,128)}, f32[256,1024]{1,0:T(8,128)}) async-done(((f32[64,3072]{1,0:T(8,128)}, f32[64,1024]{1,0:T(8,128)}, f32[64,4096]{1,0:T(8,128)}, f32[256,1024]{1,0:T(8,128)}), (f32[64,3072]{1,0:T(8,128)}, f32[64,1024]{1,0:T(8,128)}, f32[64,4096]{1,0:T(8,128)}, ...) | async-done | bytes 3145744 | tf_op jit(solution)/shard_map/psum | solution.py:285
  (152 shorter events, 104.7 us)
Async XLA Ops:
  7.2 80.1 %all-gather.6.cloned.1.call-start = ((), (), s32[]{:S(2)}) async-start(), calls=%async_computation.8 | async-start | bytes 6684672 | tf_op jit(solution)/shard_map/all_gather | solution.py:110
  7.9 160.0 %all-gather.8.cloned.1.call-start = ((), (), s32[]{:S(2)}) async-start(), calls=%async_computation.9 | async-start | bytes 2228224 | tf_op jit(solution)/shard_map/all_gather | solution.py:113
  8.7 185.0 %all-gather.10.cloned.1.call-start = ((), (), s32[]{:S(2)}) async-start(), calls=%async_computation.10 | async-start | bytes 8912896 | tf_op jit(solution)/shard_map/all_gather | solution.py:118
  9.4 259.5 %all-gather.12.cloned.1.call-start = ((), (), s32[]{:S(2)}) async-start(), calls=%async_computation.11 | async-start | bytes 8912896 | tf_op jit(solution)/shard_map/all_gather | solution.py:120
  93.5 9.4 copy-start.14
  99.0 19.1 %all-to-all-start = ((bf16[256,3,2,512]{3,0,1,2:T(8,128)(2,1)}), bf16[256,3,2,512]{3,0,1,2:T(8,128)(2,1)S(1)}, u32[]{:S(2)}, u32[]{:S(2)}) async-start(bf16[256,3,2,512]{3,0,1,2:T(8,128)(2,1)} %copy.78), calls=%async_computation | async-start | bytes 3145728 | tf_op jit(solution)/shard_map/all_to_all | solution.py:157
  125.7 3.2 copy-start
  132.8 11.6 %copy-start.16 = (bf16[256]{0:T(256)(128)(2,1)S(1)}, bf16[256]{0:T(256)(128)(2,1)}, u32[]{:S(2)}) copy-start(bf16[256]{0:T(256)(128)(2,1)} %param.31) | copy-start | bytes 1540
  133.6 33.1 %copy-start.8 = (bf16[8,64,512]{2,1,0:T(8,128)(2,1)}, bf16[8,64,512]{2,1,0:T(8,128)(2,1)S(1)}, u32[]{:S(2)}) copy-start(bf16[8,64,512]{2,1,0:T(8,128)(2,1)S(1)} %convolution_convert_fusion.3) | copy-start | bytes 1572868
  134.1 33.8 %copy-start.2 = (f32[1,256,1024]{2,1,0:T(8,128)S(1)}, f32[1,256,1024]{2,1,0:T(8,128)}, u32[]{:S(2)}) copy-start(f32[1,256,1024]{2,1,0:T(8,128)} %param.18) | copy-start | bytes 3145732
  140.0 22.3 %all-to-all-start.1 = ((bf16[2,2,65536]{2,1,0:T(2,128)(2,1)}), bf16[2,2,65536]{2,1,0:T(2,128)(2,1)}, u32[]{:S(2)}, u32[]{:S(2)}) async-start(bf16[2,2,65536]{2,1,0:T(2,128)(2,1)} %reshape.233), calls=%async_computation.1 | async-start | bytes 1048576 | tf_op jit(solution)/shard_map/all_to_all | solution.py:169
  144.2 257.0 %reduce-scatter.7.cloned.1.call-start = ((), (), s32[]{:S(2)}) async-start(), calls=%async_computation.13 | async-start | bytes 4456448 | tf_op jit(solution)/shard_map/reduce_scatter | solution.py:257
  268.9 6.9 copy-start.5
  275.8 6.9 copy-start.10
  275.8 6.9 copy-start.7
  275.8 6.9 copy-start.11
  275.8 6.9 copy-start.13
  275.8 8.4 copy-start.15
  291.6 216.1 %reduce-scatter.5.cloned.1.call-start = ((), (), s32[]{:S(2)}) async-start(), calls=%async_computation.12 | async-start | bytes 13369344 | tf_op jit(solution)/shard_map/reduce_scatter | solution.py:254
  306.7 10.5 %copy-start.9 = (bf16[8,64,512]{2,1,0:T(8,128)(2,1)S(1)}, bf16[8,64,512]{2,1,0:T(8,128)(2,1)}, u32[]{:S(2)}) copy-start(bf16[8,64,512]{2,1,0:T(8,128)(2,1)} %copy-done.8) | copy-start | bytes 1572868
  376.0 314.1 %reduce-scatter.9.cloned.1.call-start = ((), (), s32[]{:S(2)}) async-start(), calls=%async_computation.14 | async-start | bytes 17825792 | tf_op jit(solution)/shard_map/reduce_scatter | solution.py:262
  388.8 483.5 %reduce-scatter.11.cloned.1.call-start = ((), (), s32[]{:S(2)}) async-start(), calls=%async_computation.15 | async-start | bytes 17825792 | tf_op jit(solution)/shard_map/reduce_scatter | solution.py:264
  401.2 559.3 %all-reduce.27.cloned.1.call-start = ((), (), s32[]{:S(2)}) async-start(), calls=%async_computation.16 | async-start | bytes 6291456 | tf_op jit(solution)/shard_map/psum | solution.py:285
  960.5 6.1 copy-start.12
  (4 other events, 5.8 us)
Sparse Core Ops, SparseCore 0:
  10.3 65.0 all-gather.5
  77.6 40.0 all-gather.7
  119.9 73.7 all-gather.9
  195.7 73.1 all-gather.11
  291.7 70.7 reduce-scatter.6
  376.1 131.5 reduce-scatter.4
  512.4 177.6 reduce-scatter.8
  694.7 177.4 reduce-scatter.10
  874.9 85.5 all-reduce.26
where the time goes:
time: 981 us; the launch traced here: 974 us
  waiting for transfers between devices  589 us (60%)
  blocking collectives  186 us (19%)
  matrix products  95.7 us (10%)
  local copies, waits for them, and re-layouts  60.6 us (6%)
  other arithmetic  18.1 us (2%)
  between operations  16.5 us (2%)
    reduce_scatter x1, waiting for transfers between devices, on_device(): lax.psum_scatter(grad_expand, 'fsdp', scatter_dimension=0, tiled=True)  182 us
    reduce_scatter x1, waiting for transfers between devices, on_device(): lax.psum_scatter(grad_reduce, 'fsdp', scatter_dimension=0, tiled=True)  182 us
    unnamed x2, blocking collectives  124 us
    reduce_scatter x1, waiting for transfers between devices, on_device(): lax.psum_scatter(grad_qkv, 'fsdp', scatter_dimension=0, tiled=True)  106 us
    all_gather x1, waiting for transfers between devices, on_device(): lax.all_gather(fc2_weight, 'fsdp', axis=0, tiled=True)  67.1 us
    unnamed x75, local copies, waits for them, and re-layouts  34.6 us
    all_to_all x1, blocking collectives, on_device(): lax.all_to_all(stacked, 'seq', split_axis=0, concat_axis=2, tiled=True)  27.3 us
    all_gather x1, waiting for transfers between devices, on_device(): lax.all_gather(fc1_weight, 'fsdp', axis=0, tiled=True)  21.2 us
  transfers between devices with their start and end apart: 11, of which 7 were waited for; matrix products, arithmetic and copies ran while one was open for 14% of the time, Pallas kernels for 0%

commit v1 on v0

--- a/solution.py
+++ b/solution.py
@@ -82,6 +82,64 @@
         "hqk,qhd->khd", grad_scores, query, preferred_element_type=jnp.float32
     ).astype(jnp.bfloat16)
     return (grad_query, grad_keys, grad_values)
+
+
+def level_pairs(bit):
+    count = lax.axis_size("fsdp")
+    return [(i, i ^ (1 << bit)) for i in range(count)]
+
+
+def my_bit(bit):
+    return (lax.axis_index("fsdp") >> bit) & 1
+
+
+def levels():
+    return int(lax.axis_size("fsdp")).bit_length() - 1
+
+
+def gather_by_doubling(block):
+    shape = block.shape
+    held, done = block, []
+    for bit in list(range(2, levels())) + [1, 0]:
+        other = lax.ppermute(held, "fsdp", level_pairs(bit))
+        mine_first = my_bit(bit) == 0
+        place = sum(1 for earlier in done if earlier > bit)
+        held = jnp.stack(
+            [jnp.where(mine_first, held, other), jnp.where(mine_first, other, held)], axis=place
+        )
+        done.append(bit)
+    return held.reshape((-1,) + shape[1:])
+
+
+def scatter_by_halving(terms):
+    count, top = lax.axis_size("fsdp"), levels()
+    rows = terms.shape[0] // count
+    held = terms.reshape((2,) * top + (rows,) + terms.shape[1:])
+    left = list(range(top))[::-1]
+    total = None
+    for bit in [0, 1] + list(range(2, top))[::-1]:
+        place = left.index(bit)
+        mine = my_bit(bit)
+        sent = lax.dynamic_index_in_dim(held, 1 - mine, place, keepdims=False)
+        kept = lax.dynamic_index_in_dim(held, mine, place, keepdims=False)
+        other = lax.ppermute(sent, "fsdp", level_pairs(bit))
+        total = wide(kept) + wide(other)
+        held = total.astype(jnp.bfloat16)
+        left.remove(bit)
+    return held
+
+
+def owned_rows(terms, by_halving):
+    if by_halving:
+        part = scatter_by_halving(terms)
+    else:
+        part = lax.psum_scatter(terms, "fsdp", scatter_dimension=0, tiled=True)
+    count = lax.axis_size("seq")
+    total = wide(part)
+    for step in range(1, count):
+        other = lax.ppermute(part, "seq", [(i, (i + step) % count) for i in range(count)])
+        total = total + wide(other)
+    return total
 
 
 def on_device(
@@ -104,40 +162,48 @@
     second_scale,
     cotangent,
 ):
-    gathered = (
-        lax.all_gather(first_gain, "fsdp", axis=0, tiled=True),
-        lax.all_gather(first_shift, "fsdp", axis=0, tiled=True),
-        lax.all_gather(qkv_weight, "fsdp", axis=0, tiled=True),
-        lax.all_gather(query_bias, "fsdp", axis=0, tiled=True),
-        lax.all_gather(value_bias, "fsdp", axis=0, tiled=True),
-        lax.all_gather(proj_weight, "fsdp", axis=0, tiled=True),
-        lax.all_gather(proj_bias, "fsdp", axis=0, tiled=True),
-        lax.all_gather(first_scale, "fsdp", axis=0, tiled=True),
-        lax.all_gather(second_gain, "fsdp", axis=0, tiled=True),
-        lax.all_gather(second_shift, "fsdp", axis=0, tiled=True),
-        lax.all_gather(fc1_weight, "fsdp", axis=0, tiled=True),
-        lax.all_gather(fc1_bias, "fsdp", axis=0, tiled=True),
-        lax.all_gather(fc2_weight, "fsdp", axis=0, tiled=True),
-        lax.all_gather(fc2_bias, "fsdp", axis=0, tiled=True),
-        lax.all_gather(second_scale, "fsdp", axis=0, tiled=True),
-    )
+    rows = first_gain.shape[0]
+    vectors = (
+        first_gain,
+        first_shift,
+        query_bias,
+        value_bias,
+        proj_bias,
+        first_scale,
+        second_gain,
+        second_shift,
+        fc2_bias,
+        second_scale,
+    )
+    ratio = fc1_bias.shape[0] // rows
+    columns = jnp.concatenate(
+        [jnp.stack(vectors, axis=1), fc1_bias.reshape(rows, ratio)], axis=1
+    )
+    spare = 128 - columns.shape[1]
+    columns = jnp.pad(columns, ((0, 0), (0, spare)))
+    joint_all = lax.all_gather(
+        jnp.concatenate([qkv_weight, columns], axis=1), "fsdp", axis=0, tiled=True
+    )
+    proj_full = lax.all_gather(proj_weight, "fsdp", axis=0, tiled=True)
+    expand_full = lax.all_gather(fc1_weight, "fsdp", axis=0, tiled=True)
+    reduce_full = gather_by_doubling(fc2_weight)
+    joint_cols = qkv_weight.shape[1]
+    joint_full = joint_all[:, :joint_cols]
+    small = joint_all[:, joint_cols:]
+    small_t = small.T
     (
         gain_one,
         shift_one,
-        joint_full,
         qbias_full,
         vbias_full,
-        proj_full,
         pbias_full,
         scale_one,
         gain_two,
         shift_two,
-        expand_full,
-        ebias_full,
-        reduce_full,
         rbias_full,
         scale_two,
-    ) = gathered
+    ) = tuple(small_t[i] for i in range(10))
+    ebias_full = small[:, 10 : 10 + ratio].reshape(-1)
     width = joint_full.shape[0]
     tokens = block_input[0]
     count = tokens.shape[0]
@@ -178,52 +244,41 @@
     hidden = smooth_gate(pre).astype(jnp.bfloat16)
     branch = jnp.dot(hidden, reduce_full, preferred_element_type=jnp.float32) + wide(rbias_full)
     result = resid + wide(scale_two) * branch
-    again = (
-        lax.all_gather(qkv_weight, "fsdp", axis=0, tiled=True),
-        lax.all_gather(proj_weight, "fsdp", axis=0, tiled=True),
-        lax.all_gather(first_gain, "fsdp", axis=0, tiled=True),
-        lax.all_gather(first_scale, "fsdp", axis=0, tiled=True),
-        lax.all_gather(second_gain, "fsdp", axis=0, tiled=True),
-        lax.all_gather(second_scale, "fsdp", axis=0, tiled=True),
-        lax.all_gather(fc1_weight, "fsdp", axis=0, tiled=True),
-        lax.all_gather(fc2_weight, "fsdp", axis=0, tiled=True),
-    )
-    (
-        back_joint,
-        back_proj,
-        back_gain1,
-        back_scale1,
-        back_gain2,
-        back_scale2,
-        back_expand,
-        back_reduce,
-    ) = again
     grad_out = cotangent[0]
     grad_scale2 = jnp.sum(grad_out * branch, axis=0)
-    grad_branch = wide(back_scale2) * grad_out
+    grad_branch = wide(scale_two) * grad_out
     grad_bias2 = jnp.sum(grad_branch, axis=0)
     branch_low = grad_branch.astype(jnp.bfloat16)
     grad_reduce = jnp.einsum("tf,td->fd", hidden, branch_low, preferred_element_type=jnp.float32)
+    reduce_low = grad_reduce.astype(jnp.bfloat16)
+    reduce_low, branch_low = lax.optimization_barrier((reduce_low, branch_low))
+    own_fc2 = owned_rows(reduce_low, True)
     grad_hidden = jnp.einsum(
-        "td,fd->tf", branch_low, back_reduce, preferred_element_type=jnp.float32
+        "td,fd->tf", branch_low, reduce_full, preferred_element_type=jnp.float32
     )
     grad_pre = grad_hidden * gate_slope(pre)
     grad_bias1 = jnp.sum(grad_pre, axis=0)
     pre_low = grad_pre.astype(jnp.bfloat16)
     grad_expand = jnp.einsum("td,tf->df", act2, pre_low, preferred_element_type=jnp.float32)
-    grad_act2 = jnp.einsum("tf,df->td", pre_low, back_expand, preferred_element_type=jnp.float32)
+    expand_low = grad_expand.astype(jnp.bfloat16)
+    expand_low, pre_low = lax.optimization_barrier((expand_low, pre_low))
+    own_fc1 = owned_rows(expand_low, False)
+    grad_act2 = jnp.einsum("tf,df->td", pre_low, expand_full, preferred_element_type=jnp.float32)
     grad_gain2 = jnp.sum(grad_act2 * unit2, axis=0)
     grad_shift2 = jnp.sum(grad_act2, axis=0)
-    grad_resid = grad_out + normalize_back(grad_act2, unit2, inv2, wide(back_gain2))
+    grad_resid = grad_out + normalize_back(grad_act2, unit2, inv2, wide(gain_two))
     grad_scale1 = jnp.sum(grad_resid * mixed, axis=0)
-    grad_mixed = wide(back_scale1) * grad_resid
+    grad_mixed = wide(scale_one) * grad_resid
     grad_pbias = jnp.sum(grad_mixed, axis=0)
     mixed_low = grad_mixed.astype(jnp.bfloat16)
     grad_proj = jnp.einsum(
         "td,te->de", attended_flat, mixed_low, preferred_element_type=jnp.float32
     )
+    proj_low = grad_proj.astype(jnp.bfloat16)
+    proj_low, mixed_low = lax.optimization_barrier((proj_low, mixed_low))
+    own_proj = owned_rows(proj_low, False)
     grad_attended = jnp.einsum(
-        "te,de->td", mixed_low, back_proj, preferred_element_type=jnp.float32
+        "te,de->td", mixed_low, proj_full, preferred_element_type=jnp.float32
     ).astype(jnp.bfloat16)
     grad_spread = lax.all_to_all(
         grad_attended.reshape(count, seq_count, local_cols),
@@ -244,28 +299,45 @@
     grad_qbias = jnp.sum(wide(grad_joint[:, :width]), axis=0)
     grad_vbias = jnp.sum(wide(grad_joint[:, 2 * width :]), axis=0)
     grad_qkv = jnp.einsum("td,te->de", act1, grad_joint, preferred_element_type=jnp.float32)
-    grad_act1 = jnp.einsum("te,de->td", grad_joint, back_joint, preferred_element_type=jnp.float32)
+    grad_act1 = jnp.einsum("te,de->td", grad_joint, joint_full, preferred_element_type=jnp.float32)
     grad_gain1 = jnp.sum(grad_act1 * unit1, axis=0)
     grad_shift1 = jnp.sum(grad_act1, axis=0)
-    grad_in = grad_resid + normalize_back(grad_act1, unit1, inv1, wide(back_gain1))
-    owned = (
-        lax.psum_scatter(grad_gain1, "fsdp", scatter_dimension=0, tiled=True),
-        lax.psum_scatter(grad_shift1, "fsdp", scatter_dimension=0, tiled=True),
-        lax.psum_scatter(grad_qkv, "fsdp", scatter_dimension=0, tiled=True),
-        lax.psum_scatter(grad_qbias, "fsdp", scatter_dimension=0, tiled=True),
-        lax.psum_scatter(grad_vbias, "fsdp", scatter_dimension=0, tiled=True),
-        lax.psum_scatter(grad_proj, "fsdp", scatter_dimension=0, tiled=True),
-        lax.psum_scatter(grad_pbias, "fsdp", scatter_dimension=0, tiled=True),
-        lax.psum_scatter(grad_scale1, "fsdp", scatter_dimension=0, tiled=True),
-        lax.psum_scatter(grad_gain2, "fsdp", scatter_dimension=0, tiled=True),
-        lax.psum_scatter(grad_shift2, "fsdp", scatter_dimension=0, tiled=True),
-        lax.psum_scatter(grad_expand, "fsdp", scatter_dimension=0, tiled=True),
-        lax.psum_scatter(grad_bias1, "fsdp", scatter_dimension=0, tiled=True),
-        lax.psum_scatter(grad_reduce, "fsdp", scatter_dimension=0, tiled=True),
-        lax.psum_scatter(grad_bias2, "fsdp", scatter_dimension=0, tiled=True),
-        lax.psum_scatter(grad_scale2, "fsdp", scatter_dimension=0, tiled=True),
-    )
+    grad_in = grad_resid + normalize_back(grad_act1, unit1, inv1, wide(gain_one))
+    sums = jnp.stack(
+        (
+            grad_gain1,
+            grad_shift1,
+            grad_qbias,
+            grad_vbias,
+            grad_pbias,
+            grad_scale1,
+            grad_gain2,
+            grad_shift2,
+            grad_bias2,
+            grad_scale2,
+        ),
+        axis=1,
+    )
+    sums = jnp.concatenate([sums, grad_bias1.reshape(width, ratio)], axis=1)
+    sums = jnp.pad(sums, ((0, 0), (0, spare)))
+    last = jnp.concatenate([grad_qkv.astype(jnp.bfloat16), sums.astype(jnp.bfloat16)], axis=1)
+    own_last = owned_rows(last, True)
+    own_qkv = own_last[:, :joint_cols]
+    own_small = own_last[:, joint_cols:].T
     (
+        own_g1,
+        own_s1,
+        own_qb,
+        own_vb,
+        own_pb,
+        own_l1,
+        own_g2,
+        own_s2,
+        own_b2,
+        own_l2,
+    ) = tuple(own_small[i] for i in range(10))
+    own_b1 = own_last[:, joint_cols + 10 : joint_cols + 10 + ratio].reshape(-1)
+    summed = (
         own_g1,
         own_s1,
         own_qkv,
@@ -281,26 +353,6 @@
         own_fc2,
         own_b2,
         own_l2,
-    ) = owned
-    summed = lax.psum(
-        (
-            own_g1,
-            own_s1,
-            own_qkv,
-            own_qb,
-            own_vb,
-            own_proj,
-            own_pb,
-            own_l1,
-            own_g2,
-            own_s2,
-            own_fc1,
-            own_b1,
-            own_fc2,
-            own_b2,
-            own_l2,
-        ),
-        "seq",
     )
     return (
         result[None],

time: 981 us -> 643 us (0.66)
  waiting for transfers between devices: 589 us -> 367 us
  blocking collectives: 186 us -> 11.5 us
  other arithmetic: 18.1 us -> 57.8 us
  matrix products: 95.7 us -> 73.2 us
  starting transfers between devices: 8.68 us -> 29.9 us
  local copies, waits for them, and re-layouts: 60.6 us -> 81.3 us
    reduce_scatter x4 -> x2, waiting for transfers between devices: 471 us -> 0.01 us  [owned_rows(): part = lax.psum_scatter(terms, 'fsdp', scatter_dimension=0, tiled=True)]
    ppermute x0 -> x16, waiting for transfers between devices: none -> 333 us  [the longest x8 171 us: scatter_by_halving(): other = lax.ppermute(sent, 'fsdp', level_pairs(bit))]
    unnamed x2 -> x0, blocking collectives: 124 us -> none
    all_gather x4 -> x3, waiting for transfers between devices: 88.3 us -> 0.06 us  [the longest x1 0.02 us: on_device(): proj_full = lax.all_gather(proj_weight, 'fsdp', axis=0, tiled=True)]
    all_to_all x1 -> x0, blocking collectives: 27.3 us -> none  [on_device(): lax.all_to_all(stacked, 'seq', split_axis=0, concat_axis=2, tiled=True)]
    unnamed x75 -> x71, local copies, waits for them, and re-layouts: 34.6 us -> 12.7 us
    another operation x0 -> x8, other arithmetic: none -> 19.3 us  [gather_by_doubling(): jnp.stack([jnp.where(mine_first, held, other), jnp.where(mine_first, othe...]
    all_to_all x0 -> x1, waiting for transfers between devices: none -> 17.9 us  [on_device(): lax.all_to_all(stacked, 'seq', split_axis=0, concat_axis=2, tiled=True)]
  transfers between devices with their start and end apart: 11 -> 24, of which waited for: 7 -> 14; matrix products, arithmetic and copies ran while one was open for 14% -> 20% of each run, Pallas kernels for 0% -> 0%
where the time goes in v1:
time: 643 us; the launch traced here: 636 us
  waiting for transfers between devices  367 us (57%)
  local copies, waits for them, and re-layouts  81.3 us (13%)
  matrix products  73.2 us (11%)
  other arithmetic  57.8 us (9%)
  starting transfers between devices  29.9 us (5%)
  between operations  14.8 us (2%)
  blocking collectives  11.5 us (2%)
    ppermute x8, waiting for transfers between devices, scatter_by_halving(): other = lax.ppermute(sent, 'fsdp', level_pairs(bit))  171 us
    ppermute x4, waiting for transfers between devices, gather_by_doubling(): other = lax.ppermute(held, 'fsdp', level_pairs(bit))  143 us
    another operation x8, other arithmetic, gather_by_doubling(): jnp.stack([jnp.where(mine_first, held, other), jnp.where(mine_first, othe...  19.3 us
    ppermute x4, waiting for transfers between devices, owned_rows(): lax.ppermute(part, 'seq', [(i, (i + step) % count) for i in range(count)])  19.2 us
    all_to_all x1, waiting for transfers between devices, on_device(): lax.all_to_all(stacked, 'seq', split_axis=0, concat_axis=2, tiled=True)  17.9 us
    convert_element_type x8, other arithmetic, scatter_by_halving(): held = total.astype(jnp.bfloat16)  15.7 us
    all_to_all x1, waiting for transfers between devices, on_device(): lax.all_to_all(joint.reshape(count, 3, seq_count, local_cols), 'seq', spl...  14.3 us
  transfers between devices with their start and end apart: 24, of which 14 were waited for; matrix products, arithmetic and copies ran while one was open for 20% of the time, Pallas kernels for 0%

profile of v1, /device:TPU:0, one launch (start us, length us, event | category | flops | bytes accessed | tf_op | source)
XLA Modules:
  0.0 635.6 jit_solution(11357309836302949958)
XLA Ops:
  16.1 18.9 %collective-permute-done = bf16[256,1024]{1,0:T(8,128)(2,1)S(1)} collective-permute-done((bf16[256,1024]{1,0:T(8,128)(2,1)}, bf16[256,1024]{1,0:T(8,128)(2,1)S(1)}, u32[]{:S(2)}, u32[]{:S(2)}) %collective-permute-start) | collective-permute-done | bytes 524320 | tf_op jit(solution)/shard_map/ppermute | solution.py:104
  36.3 5.7 collective-permute-start.1
  41.9 72.3 %collective-permute-done.1 = bf16[2,256,1024]{2,1,0:T(8,128)(2,1)S(1)} collective-permute-done((bf16[2,256,1024]{2,1,0:T(8,128)(2,1)S(1)}, bf16[2,256,1024]{2,1,0:T(8,128)(2,1)S(1)}, u32[]{:S(2)}, u32[]{:S(2)}) %collective-permute-start.1) | collective-permute-done | bytes 1048608 | tf_op jit(solution)/shard_map/ppermute | solution.py:104
  117.2 52.0 %collective-permute-done.2 = bf16[2,2,256,1024]{3,2,1,0:T(8,128)(2,1)} collective-permute-done((bf16[2,2,256,1024]{3,2,1,0:T(8,128)(2,1)S(1)}, bf16[2,2,256,1024]{3,2,1,0:T(8,128)(2,1)}, u32[]{:S(2)}, u32[]{:S(2)}) %collective-permute-start.2) | collective-permute-done | bytes 2097184 | tf_op jit(solution)/shard_map/ppermute | solution.py:104
  177.1 5.8 fusion.18
  195.9 5.8 select_bitcast_fusion.1
  201.7 14.3 %all-to-all-done = bf16[256,3,2,512]{3,0,1,2:T(8,128)(2,1)} async-done(((bf16[256,3,2,512]{3,0,1,2:T(8,128)(2,1)}), bf16[256,3,2,512]{3,0,1,2:T(8,128)(2,1)}, u32[]{:S(2)}, u32[]{:S(2)}) %all-to-all-start) | async-done | bytes 1572896 | tf_op jit(solution)/shard_map/all_to_all | solution.py:223
  240.2 7.5 %pad_maximum_fusion = bf16[2,2,2,2,256,1024]{5,4,3,2,1,0:T(8,128)(2,1)} fusion(bf16[2,2,2,1,256,1024]{5,4,3,2,1,0:T(8,128)(2,1)} %get-tuple-element.69, bf16[2,2,2,1,256,1024]{5,4,3,2,1,0:T(8,128)(2,1)} %get-tuple-element.68), kind=kLoop, calls=%fused_computation.2 | loop fusion | flops 4194304 | bytes 16777216 | tf_op jit(solution)/shard_map/stack | solution.py:107
  260.9 7.0 %fusion.26 = (bf16[1024]{0:T(1024)(128)(2,1)S(1)}, bf16[1024]{0:T(1024)(128)(2,1)S(1)}, bf16[256,1024]{1,0:T(8,128)(2,1)S(1)}, f32[1,256,1024]{2,1,0:T(8,128)}) fusion(f32[1,256,1024]{2,1,0:T(8,128)S(1)} %copy-done.19, f32[1024]{0:T(1024)S(1)} %get-tuple-element.43, f32[256,1024]{1,0:T(8,128)S(1)} %get-tuple-element.65, f32[1024]{0:T(1024)S(1)} %get-tuple-element.44, ...), kind=kOutput, calls=%fused_computation.69 | convolution fusion | flops 2149578752 | bytes 14168064 | tf_op jit(solution)/shard_map/dot_general | solution.py:245
  279.3 5.8 convolution_convert_fusion
  285.1 6.9 %multiply_reduce_fusion = (bf16[1024]{0:T(1024)(128)(2,1)S(1)}, f32[256]{0:T(256)S(1)}, f32[256]{0:T(256)S(1)}, bf16[1024]{0:T(1024)(128)(2,1)S(1)}, f32[256,1024]{1,0:T(8,128)S(1)}) fusion(f32[256,1024]{1,0:T(8,128)S(1)} %get-tuple-element.65, f32[256]{0:T(256)S(1)} %add_rsqrt_fusion, f32[256]{0:T(256)S(1)} %broadcast_multiply_fusion.4, ...), kind=kOutput, calls=%fused_computation.75 | convolution fusion | flops 2149840384 | bytes 12595200 | tf_op jit(solution)/shard_map/tf,df->td/dot_general | solution.py:266
  297.9 11.5 %all_to_all.60 = bf16[256,2,512]{2,0,1:T(8,128)(2,1)} all-to-all(bf16[256,2,512]{2,0,1:T(8,128)(2,1)S(1)} %bitcast.214), channel_id=1, replica_groups=mesh['seq'=2,'fsdp'=16] {'seq'}, dimensions={1} | all-to-all | bytes 1048576 | tf_op jit(solution)/shard_map/all_to_all | solution.py:283
  334.8 5.7 pad_maximum_fusion.3
  350.4 17.9 %all-to-all-done.3 = bf16[512,3,1,512]{3,1,2,0:T(4,128)(2,1)S(1)} async-done(((bf16[512,3,1,512]{3,1,2,0:T(4,128)(2,1)}), bf16[512,3,1,512]{3,1,2,0:T(4,128)(2,1)S(1)}, u32[]{:S(2)}, u32[]{:S(2)}) %all-to-all-start.3) | async-done | bytes 1572896 | tf_op jit(solution)/shard_map/all_to_all | solution.py:297
  372.0 5.8 multiply_reduce_fusion.2
  391.9 6.9 %constant_dynamic-slice_fusion.1 = (bf16[2,2,2,1,256,1024]{5,4,3,2,1,0:T(8,128)(2,1)}, bf16[2,2,2,1,256,1024]{5,4,3,2,1,0:T(8,128)(2,1)S(1)}) fusion(bf16[2,2,2,2,256,1024]{5,4,3,2,1,0:T(8,128)(2,1)} %bitcast.197, s32[]{:T(128)S(6)} %select_n.106, s32[]{:T(128)S(6)} %select_n.107), kind=kLoop, calls=%fused_computation.152 | loop fusion | bytes 16777224 | tf_op jit(solution)/shard_map/jit(dynamic_index_in_dim)/dynamic_slice | solution.py:124
  417.3 29.0 %collective-permute-done.5 = bf16[2,2,64,3200]{3,2,1,0:T(8,128)(2,1)} collective-permute-done((bf16[2,2,64,3200]{3,2,1,0:T(8,128)(2,1)}, bf16[2,2,64,3200]{3,2,1,0:T(8,128)(2,1)}, u32[]{:S(2)}, u32[]{:S(2)}) %collective-permute-start.5) | collective-permute-done | bytes 1638432 | tf_op jit(solution)/shard_map/ppermute | solution.py:125
  449.4 52.2 %collective-permute-done.12 = bf16[2,2,256,1024]{3,2,1,0:T(8,128)(2,1)} collective-permute-done((bf16[2,2,256,1024]{3,2,1,0:T(8,128)(2,1)S(1)}, bf16[2,2,256,1024]{3,2,1,0:T(8,128)(2,1)}, u32[]{:S(2)}, u32[]{:S(2)}) %collective-permute-start.12) | collective-permute-done | bytes 2097184 | tf_op jit(solution)/shard_map/ppermute | solution.py:125
  505.3 36.7 %collective-permute-done.6 = bf16[2,64,3200]{2,1,0:T(8,128)(2,1)S(1)} collective-permute-done((bf16[2,64,3200]{2,1,0:T(8,128)(2,1)S(1)}, bf16[2,64,3200]{2,1,0:T(8,128)(2,1)S(1)}, u32[]{:S(2)}, u32[]{:S(2)}) %collective-permute-start.6) | collective-permute-done | bytes 819232 | tf_op jit(solution)/shard_map/ppermute | solution.py:125
  545.7 28.8 %collective-permute-done.13 = bf16[2,256,1024]{2,1,0:T(8,128)(2,1)} collective-permute-done((bf16[2,256,1024]{2,1,0:T(8,128)(2,1)}, bf16[2,256,1024]{2,1,0:T(8,128)(2,1)}, u32[]{:S(2)}, u32[]{:S(2)}) %collective-permute-start.13) | collective-permute-done | bytes 1048608 | tf_op jit(solution)/shard_map/ppermute | solution.py:125
  576.3 13.9 %collective-permute-done.7 = bf16[64,3200]{1,0:T(8,128)(2,1)S(1)} collective-permute-done((bf16[64,3200]{1,0:T(8,128)(2,1)}, bf16[64,3200]{1,0:T(8,128)(2,1)S(1)}, u32[]{:S(2)}, u32[]{:S(2)}) %collective-permute-start.7) | collective-permute-done | bytes 409632 | tf_op jit(solution)/shard_map/ppermute | solution.py:125
  591.4 10.0 %collective-permute-done.14 = bf16[256,1024]{1,0:T(8,128)(2,1)S(1)} collective-permute-done((bf16[256,1024]{1,0:T(8,128)(2,1)S(1)}, bf16[256,1024]{1,0:T(8,128)(2,1)S(1)}, u32[]{:S(2)}, u32[]{:S(2)}) %collective-permute-start.14) | collective-permute-done | bytes 524320 | tf_op jit(solution)/shard_map/ppermute | solution.py:125
  606.3 10.1 %collective-permute-done.15 = bf16[256,1024]{1,0:T(8,128)(2,1)S(1)} collective-permute-done((bf16[256,1024]{1,0:T(8,128)(2,1)S(1)}, bf16[256,1024]{1,0:T(8,128)(2,1)S(1)}, u32[]{:S(2)}, u32[]{:S(2)}) %collective-permute-start.15) | collective-permute-done | bytes 524320 | tf_op jit(solution)/shard_map/ppermute | solution.py:140
  617.6 9.2 %collective-permute-done.10 = bf16[64,4096]{1,0:T(8,128)(2,1)S(1)} collective-permute-done((bf16[64,4096]{1,0:T(8,128)(2,1)}, bf16[64,4096]{1,0:T(8,128)(2,1)S(1)}, u32[]{:S(2)}, u32[]{:S(2)}) %collective-permute-start.10) | collective-permute-done | bytes 524320 | tf_op jit(solution)/shard_map/ppermute | solution.py:140
  (213 shorter events, 181.2 us)
Async XLA Ops:
  7.2 167.4 %all-gather.4.cloned.1.call-start = ((), (), s32[]{:S(2)}) async-start(), calls=%async_computation.6 | async-start | bytes 6963200 | tf_op jit(solution)/shard_map/all_gather | solution.py:184
  11.5 240.2 %all-gather.6.cloned.1.call-start = ((), (), s32[]{:S(2)}) async-start(), calls=%async_computation.7 | async-start | bytes 2228224 | tf_op jit(solution)/shard_map/all_gather | solution.py:187
  12.3 243.1 %all-gather.8.cloned.1.call-start = ((), (), s32[]{:S(2)}) async-start(), calls=%async_computation.8 | async-start | bytes 8912896 | tf_op jit(solution)/shard_map/all_gather | solution.py:188
  13.0 22.0 %collective-permute-start = (bf16[256,1024]{1,0:T(8,128)(2,1)}, bf16[256,1024]{1,0:T(8,128)(2,1)S(1)}, u32[]{:S(2)}, u32[]{:S(2)}) collective-permute-start(bf16[256,1024]{1,0:T(8,128)(2,1)} %param.32), channel_id=1, source_target_pairs={{0,4},{1,5},{2,6},{3,7},{4,0},{5,1},{6,2},{7,3},{8,12},{9,13},{10,... | collective-permute-start | bytes 1572872 | tf_op jit(solution)/shard_map/ppermute | solution.py:104
  36.3 78.0 %collective-permute-start.1 = (bf16[2,256,1024]{2,1,0:T(8,128)(2,1)S(1)}, bf16[2,256,1024]{2,1,0:T(8,128)(2,1)S(1)}, u32[]{:S(2)}, u32[]{:S(2)}) collective-permute-start(bf16[2,256,1024]{2,1,0:T(8,128)(2,1)S(1)} %pad_maximum_fusion.4), channel_id=1, source_target_pairs={{0,8},{1,9},{2,10},{3,11},{4,12},{5,13},{6,14},{7,15},{8,0},{9,1},... | collective-permute-start | bytes 3145736 | tf_op jit(solution)/shard_map/ppermute | solution.py:104
  115.5 53.6 %collective-permute-start.2 = (bf16[2,2,256,1024]{3,2,1,0:T(8,128)(2,1)S(1)}, bf16[2,2,256,1024]{3,2,1,0:T(8,128)(2,1)}, u32[]{:S(2)}, u32[]{:S(2)}) collective-permute-start(bf16[2,2,256,1024]{3,2,1,0:T(8,128)(2,1)S(1)} %pad_maximum_fusion.2), channel_id=1, source_target_pairs={{0,2},{1,3},{2,0},{3,1},{4,6},{5,7},{6,4},{7,5},{8,10},{9,11},{10,... | collective-permute-start | bytes 6291464 | tf_op jit(solution)/shard_map/ppermute | solution.py:104
  174.1 21.8 %collective-permute-start.3 = (bf16[2,2,2,256,1024]{4,3,2,1,0:T(8,128)(2,1)}, bf16[2,2,2,256,1024]{4,3,2,1,0:T(8,128)(2,1)}, u32[]{:S(2)}, u32[]{:S(2)}) collective-permute-start(bf16[2,2,2,256,1024]{4,3,2,1,0:T(8,128)(2,1)} %pad_maximum_fusion.1), channel_id=1, source_target_pairs={{0,1},{1,0},{2,3},{3,2},{4,5},{5,4},{6,7},{7,6},{8,9},{9,8},{10,11... | collective-permute-start | bytes 12582920 | tf_op jit(solution)/shard_map/ppermute | solution.py:104
  190.7 25.4 %all-to-all-start = ((bf16[256,3,2,512]{3,0,1,2:T(8,128)(2,1)}), bf16[256,3,2,512]{3,0,1,2:T(8,128)(2,1)}, u32[]{:S(2)}, u32[]{:S(2)}) async-start(bf16[256,3,2,512]{3,0,1,2:T(8,128)(2,1)} %copy.182), calls=%async_computation | async-start | bytes 3145728 | tf_op jit(solution)/shard_map/all_to_all | solution.py:223
  236.5 12.5 %all-to-all-start.1 = ((bf16[2,2,65536]{2,1,0:T(2,128)(2,1)}), bf16[2,2,65536]{2,1,0:T(2,128)(2,1)S(1)}, u32[]{:S(2)}, u32[]{:S(2)}) async-start(bf16[2,2,65536]{2,1,0:T(2,128)(2,1)} %reshape.254), calls=%async_computation.1 | async-start | bytes 1048576 | tf_op jit(solution)/shard_map/all_to_all | solution.py:235
  340.5 27.8 %all-to-all-start.3 = ((bf16[512,3,1,512]{3,1,2,0:T(4,128)(2,1)}), bf16[512,3,1,512]{3,1,2,0:T(4,128)(2,1)S(1)}, u32[]{:S(2)}, u32[]{:S(2)}) async-start(bf16[512,3,1,512]{3,1,2,0:T(4,128)(2,1)} %pad_maximum_fusion.3), calls=%async_computation.3 | async-start | bytes 4194304 | tf_op jit(solution)/shard_map/all_to_all | solution.py:297
  344.2 201.0 %reduce-scatter.3.cloned.1.call-start = ((), (), s32[]{:S(2)}) async-start(), calls=%async_computation.9 | async-start | bytes 2228224 | tf_op jit(solution)/shard_map/reduce_scatter | solution.py:136
  350.3 253.4 %reduce-scatter.5.cloned.1.call-start = ((), (), s32[]{:S(2)}) async-start(), calls=%async_computation.10 | async-start | bytes 8912896 | tf_op jit(solution)/shard_map/reduce_scatter | solution.py:136
  391.9 10.2 %collective-permute-start.4 = (bf16[2,2,2,64,3200]{4,3,1,0,2:T(8,128)(2,1)}, bf16[2,2,2,64,3200]{4,3,1,0,2:T(8,128)(2,1)}, u32[]{:S(2)}, u32[]{:S(2)}) collective-permute-start(bf16[2,2,2,64,3200]{4,3,1,0,2:T(8,128)(2,1)} %bitcast.195), channel_id=1, source_target_pairs={{0,1},{1,0},{2,3},{3,2},{4,5},{5,4},{6,7},{7,6},{8,9},{9,8},{10,11... | collective-permute-start | bytes 9830408 | tf_op jit(solution)/shard_map/ppermute | solution.py:125
  401.5 7.6 %collective-permute-start.11 = (bf16[2,2,2,256,1024]{4,3,1,0,2:T(8,128)(2,1)}, bf16[2,2,2,256,1024]{4,3,1,0,2:T(8,128)(2,1)}, u32[]{:S(2)}, u32[]{:S(2)}) collective-permute-start(bf16[2,2,2,256,1024]{4,3,1,0,2:T(8,128)(2,1)} %bitcast.194), channel_id=1, source_target_pairs={{0,1},{1,0},{2,3},{3,2},{4,5},{5,4},{6,7},{7,6},{8,9},{9,8},{10,11... | collective-permute-start | bytes 12582920 | tf_op jit(solution)/shard_map/ppermute | solution.py:125
  407.3 39.0 %collective-permute-start.5 = (bf16[2,2,64,3200]{3,2,1,0:T(8,128)(2,1)}, bf16[2,2,64,3200]{3,2,1,0:T(8,128)(2,1)}, u32[]{:S(2)}, u32[]{:S(2)}) collective-permute-start(bf16[2,2,64,3200]{3,2,1,0:T(8,128)(2,1)} %dynamic-slice_bitcast_fusion.1), channel_id=1, source_target_pairs={{0,2},{1,3},{2,0},{3,1},{4,6},{5,7},{6,4},{7,5},{8,10},{9,11},{10,... | collective-permute-start | bytes 4915208 | tf_op jit(solution)/shard_map/ppermute | solution.py:125
  415.6 85.9 %collective-permute-start.12 = (bf16[2,2,256,1024]{3,2,1,0:T(8,128)(2,1)S(1)}, bf16[2,2,256,1024]{3,2,1,0:T(8,128)(2,1)}, u32[]{:S(2)}, u32[]{:S(2)}) collective-permute-start(bf16[2,2,256,1024]{3,2,1,0:T(8,128)(2,1)S(1)} %dynamic-slice_bitcast_fusion), channel_id=1, source_target_pairs={{0,2},{1,3},{2,0},{3,1},{4,6},{5,7},{6,4},{7,5},{8,10},{9,11},{10,... | collective-permute-start | bytes 6291464 | tf_op jit(solution)/shard_map/ppermute | solution.py:125
  449.3 92.7 %collective-permute-start.6 = (bf16[2,64,3200]{2,1,0:T(8,128)(2,1)S(1)}, bf16[2,64,3200]{2,1,0:T(8,128)(2,1)S(1)}, u32[]{:S(2)}, u32[]{:S(2)}) collective-permute-start(bf16[2,64,3200]{2,1,0:T(8,128)(2,1)S(1)} %dynamic-slice_bitcast_fusion.3), channel_id=1, source_target_pairs={{0,8},{1,9},{2,10},{3,11},{4,12},{5,13},{6,14},{7,15},{8,0},{9,1},... | collective-permute-start | bytes 2457608 | tf_op jit(solution)/shard_map/ppermute | solution.py:125
  505.3 69.2 %collective-permute-start.13 = (bf16[2,256,1024]{2,1,0:T(8,128)(2,1)}, bf16[2,256,1024]{2,1,0:T(8,128)(2,1)}, u32[]{:S(2)}, u32[]{:S(2)}) collective-permute-start(bf16[2,256,1024]{2,1,0:T(8,128)(2,1)} %dynamic-slice_bitcast_fusion.2), channel_id=1, source_target_pairs={{0,8},{1,9},{2,10},{3,11},{4,12},{5,13},{6,14},{7,15},{8,0},{9,1},... | collective-permute-start | bytes 3145736 | tf_op jit(solution)/shard_map/ppermute | solution.py:125
  543.9 46.3 %collective-permute-start.7 = (bf16[64,3200]{1,0:T(8,128)(2,1)}, bf16[64,3200]{1,0:T(8,128)(2,1)S(1)}, u32[]{:S(2)}, u32[]{:S(2)}) collective-permute-start(bf16[64,3200]{1,0:T(8,128)(2,1)} %dynamic-slice_bitcast_fusion.5), channel_id=1, source_target_pairs={{0,4},{1,5},{2,6},{3,7},{4,0},{5,1},{6,2},{7,3},{8,12},{9,13},{10,... | collective-permute-start | bytes 1228808 | tf_op jit(solution)/shard_map/ppermute | solution.py:125
  545.3 45.4 %collective-permute-start.9 = (bf16[64,1024]{1,0:T(8,128)(2,1)}, bf16[64,1024]{1,0:T(8,128)(2,1)S(1)}, u32[]{:S(2)}, u32[]{:S(2)}) collective-permute-start(bf16[64,1024]{1,0:T(8,128)(2,1)} %reduce-scatter.3.cloned.1.call-done), channel_id=1, source_target_pairs={{0,16},{16,0},{1,17},{17,1},{2,18},{18,2},{3,19},{19,3},{4,20},{20... | collective-permute-start | bytes 393224 | tf_op jit(solution)/shard_map/ppermute | solution.py:140
  576.2 25.2 %collective-permute-start.14 = (bf16[256,1024]{1,0:T(8,128)(2,1)S(1)}, bf16[256,1024]{1,0:T(8,128)(2,1)S(1)}, u32[]{:S(2)}, u32[]{:S(2)}) collective-permute-start(bf16[256,1024]{1,0:T(8,128)(2,1)S(1)} %dynamic-slice_bitcast_fusion.4), channel_id=1, source_target_pairs={{0,4},{1,5},{2,6},{3,7},{4,0},{5,1},{6,2},{7,3},{8,12},{9,13},{10,... | collective-permute-start | bytes 1572872 | tf_op jit(solution)/shard_map/ppermute | solution.py:125
  590.3 11.6 %collective-permute-start.8 = (bf16[64,3200]{1,0:T(8,128)(2,1)S(1)}, bf16[64,3200]{1,0:T(8,128)(2,1)S(1)}, u32[]{:S(2)}, u32[]{:S(2)}) collective-permute-start(bf16[64,3200]{1,0:T(8,128)(2,1)S(1)} %fusion.30), channel_id=1, source_target_pairs={{0,16},{16,0},{1,17},{17,1},{2,18},{18,2},{3,19},{19,3},{4,20},{20... | collective-permute-start | bytes 1228808 | tf_op jit(solution)/shard_map/ppermute | solution.py:140
  601.6 14.8 %collective-permute-start.15 = (bf16[256,1024]{1,0:T(8,128)(2,1)S(1)}, bf16[256,1024]{1,0:T(8,128)(2,1)S(1)}, u32[]{:S(2)}, u32[]{:S(2)}) collective-permute-start(bf16[256,1024]{1,0:T(8,128)(2,1)S(1)} %fusion.24), channel_id=1, source_target_pairs={{0,16},{16,0},{1,17},{17,1},{2,18},{18,2},{3,19},{19,3},{4,20},{20... | collective-permute-start | bytes 1572872 | tf_op jit(solution)/shard_map/ppermute | solution.py:140
  603.7 23.1 %collective-permute-start.10 = (bf16[64,4096]{1,0:T(8,128)(2,1)}, bf16[64,4096]{1,0:T(8,128)(2,1)S(1)}, u32[]{:S(2)}, u32[]{:S(2)}) collective-permute-start(bf16[64,4096]{1,0:T(8,128)(2,1)} %reduce-scatter.5.cloned.1.call-done), channel_id=1, source_target_pairs={{0,16},{16,0},{1,17},{17,1},{2,18},{18,2},{3,19},{19,3},{4,20},{20... | collective-permute-start | bytes 1572872 | tf_op jit(solution)/shard_map/ppermute | solution.py:140
  (33 other events, 1131.1 us)
Sparse Core Ops, SparseCore 0:
  11.6 103.8 all-gather.3
  117.7 46.2 all-gather.5
  166.2 73.8 all-gather.7
  350.4 62.1 reduce-scatter.2
  417.1 175.0 reduce-scatter.4

commit v2 on v1

--- a/solution.py
+++ b/solution.py
@@ -127,6 +127,11 @@
         held = total.astype(jnp.bfloat16)
         left.remove(bit)
     return held
+
+
+def after(values, earlier):
+    spot = earlier[(0,) * earlier.ndim]
+    return values + jnp.minimum(jnp.abs(spot), 0).astype(values.dtype)
 
 
 def owned_rows(terms, by_halving):
@@ -275,7 +280,7 @@
         "td,te->de", attended_flat, mixed_low, preferred_element_type=jnp.float32
     )
     proj_low = grad_proj.astype(jnp.bfloat16)
-    proj_low, mixed_low = lax.optimization_barrier((proj_low, mixed_low))
+    proj_low = after(proj_low, own_fc1)
     own_proj = owned_rows(proj_low, False)
     grad_attended = jnp.einsum(
         "te,de->td", mixed_low, proj_full, preferred_element_type=jnp.float32

time: 643 us -> 603 us (0.938)
  waiting for transfers between devices: 367 us -> 318 us
  blocking collectives: 11.5 us -> 0 us
  local copies, waits for them, and re-layouts: 81.3 us -> 90.7 us
  starting transfers between devices: 29.9 us -> 37 us
    ppermute x8, waiting for transfers between devices: 171 us -> 113 us  [scatter_by_halving(): other = lax.ppermute(sent, 'fsdp', level_pairs(bit))]
    all_to_all x1 -> x0, blocking collectives: 11.5 us -> none  [on_device(): lax.all_to_all(grad_attended.reshape(count, seq_count, local_cols), 'seq'...]
    reduce_scatter x2, waiting for transfers between devices: 0.01 us -> 9.99 us  [owned_rows(): part = lax.psum_scatter(terms, 'fsdp', scatter_dimension=0, tiled=True)]
    ppermute x4, waiting for transfers between devices: 19.2 us -> 9.71 us  [owned_rows(): lax.ppermute(part, 'seq', [(i, (i + step) % count) for i in range(count)])]
    all_to_all x0 -> x1, waiting for transfers between devices: none -> 7.56 us  [on_device(): lax.all_to_all(grad_attended.reshape(count, seq_count, local_cols), 'seq'...]
  transfers between devices with their start and end apart: 24 -> 25, of which waited for: 14 -> 14; matrix products, arithmetic and copies ran while one was open for 20% -> 28% of each run, Pallas kernels for 0% -> 0%
where the time goes in v2:
time: 603 us; the launch traced here: 596 us
  waiting for transfers between devices  318 us (53%)
  local copies, waits for them, and re-layouts  90.7 us (15%)
  matrix products  72.9 us (12%)
  other arithmetic  61 us (10%)
  starting transfers between devices  37 us (6%)
  between operations  15.7 us (3%)
    ppermute x4, waiting for transfers between devices, gather_by_doubling(): other = lax.ppermute(held, 'fsdp', level_pairs(bit))  143 us
    ppermute x8, waiting for transfers between devices, scatter_by_halving(): other = lax.ppermute(sent, 'fsdp', level_pairs(bit))  113 us
    another operation x8, other arithmetic, gather_by_doubling(): jnp.stack([jnp.where(mine_first, held, other), jnp.where(mine_first, othe...  19.3 us
    all_to_all x1, waiting for transfers between devices, on_device(): lax.all_to_all(stacked, 'seq', split_axis=0, concat_axis=2, tiled=True)  18.2 us
    convert_element_type x8, other arithmetic, scatter_by_halving(): held = total.astype(jnp.bfloat16)  16.4 us
    unnamed x71, local copies, waits for them, and re-layouts  15.7 us
    all_to_all x1, waiting for transfers between devices, on_device(): lax.all_to_all(joint.reshape(count, 3, seq_count, local_cols), 'seq', spl...  14.3 us
  transfers between devices with their start and end apart: 25, of which 14 were waited for; matrix products, arithmetic and copies ran while one was open for 28% of the time, Pallas kernels for 0%

profile of v2, /device:TPU:0, one launch (start us, length us, event | category | flops | bytes accessed | tf_op | source)
XLA Modules:
  0.0 595.7 jit_solution(7918192330781832802)
XLA Ops:
  16.1 18.9 %collective-permute-done = bf16[256,1024]{1,0:T(8,128)(2,1)S(1)} collective-permute-done((bf16[256,1024]{1,0:T(8,128)(2,1)}, bf16[256,1024]{1,0:T(8,128)(2,1)S(1)}, u32[]{:S(2)}, u32[]{:S(2)}) %collective-permute-start) | collective-permute-done | bytes 524320 | tf_op jit(solution)/shard_map/ppermute | solution.py:104
  36.3 5.7 collective-permute-start.1
  41.9 72.3 %collective-permute-done.1 = bf16[2,256,1024]{2,1,0:T(8,128)(2,1)S(1)} collective-permute-done((bf16[2,256,1024]{2,1,0:T(8,128)(2,1)S(1)}, bf16[2,256,1024]{2,1,0:T(8,128)(2,1)S(1)}, u32[]{:S(2)}, u32[]{:S(2)}) %collective-permute-start.1) | collective-permute-done | bytes 1048608 | tf_op jit(solution)/shard_map/ppermute | solution.py:104
  117.2 52.0 %collective-permute-done.2 = bf16[2,2,256,1024]{3,2,1,0:T(8,128)(2,1)} collective-permute-done((bf16[2,2,256,1024]{3,2,1,0:T(8,128)(2,1)S(1)}, bf16[2,2,256,1024]{3,2,1,0:T(8,128)(2,1)}, u32[]{:S(2)}, u32[]{:S(2)}) %collective-permute-start.2) | collective-permute-done | bytes 2097184 | tf_op jit(solution)/shard_map/ppermute | solution.py:104
  177.0 5.9 fusion.18
  195.8 5.8 select_bitcast_fusion.1
  201.6 14.3 %all-to-all-done = bf16[256,3,2,512]{3,0,1,2:T(8,128)(2,1)} async-done(((bf16[256,3,2,512]{3,0,1,2:T(8,128)(2,1)}), bf16[256,3,2,512]{3,0,1,2:T(8,128)(2,1)}, u32[]{:S(2)}, u32[]{:S(2)}) %all-to-all-start) | async-done | bytes 1572896 | tf_op jit(solution)/shard_map/all_to_all | solution.py:228
  240.4 7.5 %pad_maximum_fusion = bf16[2,2,2,2,256,1024]{5,4,3,2,1,0:T(8,128)(2,1)} fusion(bf16[2,2,2,1,256,1024]{5,4,3,2,1,0:T(8,128)(2,1)} %get-tuple-element.65, bf16[2,2,2,1,256,1024]{5,4,3,2,1,0:T(8,128)(2,1)} %get-tuple-element.64), kind=kLoop, calls=%fused_computation.2 | loop fusion | flops 4194304 | bytes 16777216 | tf_op jit(solution)/shard_map/stack | solution.py:107
  255.8 5.5 multiply_convert_fusion.1
  261.4 7.0 %fusion.26 = (bf16[1024]{0:T(1024)(128)(2,1)S(1)}, bf16[1024]{0:T(1024)(128)(2,1)S(1)}, bf16[256,1024]{1,0:T(8,128)(2,1)S(1)}, f32[1,256,1024]{2,1,0:T(8,128)}) fusion(f32[1,256,1024]{2,1,0:T(8,128)S(1)} %copy-done.23, f32[1024]{0:T(1024)S(1)} %get-tuple-element.39, f32[256,1024]{1,0:T(8,128)S(1)} %get-tuple-element.61, f32[1024]{0:T(1024)S(1)} %get-tuple-element.40, ...), kind=kOutput, calls=%fused_computation.69 | convolution fusion | flops 2149578752 | bytes 14168064 | tf_op jit(solution)/shard_map/dot_general | solution.py:250
  268.4 5.6 convolution_convert_fusion.1
  279.8 5.8 convolution_convert_fusion
  285.5 6.8 %multiply_reduce_fusion = (bf16[1024]{0:T(1024)(128)(2,1)S(1)}, f32[256]{0:T(256)S(1)}, f32[256]{0:T(256)S(1)}, bf16[1024]{0:T(1024)(128)(2,1)S(1)}, f32[256,1024]{1,0:T(8,128)S(1)}) fusion(f32[256,1024]{1,0:T(8,128)S(1)} %get-tuple-element.61, f32[256]{0:T(256)S(1)} %add_rsqrt_fusion, f32[256]{0:T(256)S(1)} %broadcast_multiply_fusion.4, ...), kind=kOutput, calls=%fused_computation.75 | convolution fusion | flops 2149840384 | bytes 12595200 | tf_op jit(solution)/shard_map/tf,df->td/dot_general | solution.py:271
  299.8 7.6 %all-to-all-done.2 = bf16[256,2,512]{2,0,1:T(8,128)(2,1)S(1)} async-done(((bf16[256,2,512]{2,0,1:T(8,128)(2,1)}), bf16[256,2,512]{2,0,1:T(8,128)(2,1)S(1)}, u32[]{:S(2)}, u32[]{:S(2)}) %all-to-all-start.2) | async-done | bytes 524320 | tf_op jit(solution)/shard_map/all_to_all | solution.py:288
  317.8 6.1 %multiply_convert_fusion = bf16[8,512,512]{1,2,0:T(8,128)(2,1)S(1)} fusion(f32[8,512,512]{1,2,0:T(8,128)} %copy-done, f32[8,512]{1,0:T(8,128)S(1)} %fusion.25, f32[8,512]{1,0:T(8,128)S(1)} %log_add_fusion, pred[512]{0:T(512)(128)(4,1)S(1)} %compare_reduce_fusion, bf16[512,8,64]{0,2,1:T(8,128)(2,1)S(1)} %copy-done.16, bf16[512,3,8,64]{0,3,2,1:T(8,128)(2,1)S(1)} %copy-done.9), kind=kOutput, calls=%fused_computation.5 | convolution fusion | flops 283115520 | bytes 13664768 | tf_op jit(solution)/shard_map/qhd,khd->hqk/dot_general | solution.py:71
  334.5 5.7 pad_maximum_fusion.3
  350.1 18.2 %all-to-all-done.3 = bf16[512,3,1,512]{3,1,2,0:T(4,128)(2,1)S(1)} async-done(((bf16[512,3,1,512]{3,1,2,0:T(4,128)(2,1)}), bf16[512,3,1,512]{3,1,2,0:T(4,128)(2,1)S(1)}, u32[]{:S(2)}, u32[]{:S(2)}) %all-to-all-start.3) | async-done | bytes 1572896 | tf_op jit(solution)/shard_map/all_to_all | solution.py:302
  371.8 5.8 multiply_reduce_fusion.2
  423.8 27.9 %collective-permute-done.5 = bf16[2,2,64,3200]{3,2,1,0:T(8,128)(2,1)} collective-permute-done((bf16[2,2,64,3200]{3,2,1,0:T(8,128)(2,1)}, bf16[2,2,64,3200]{3,2,1,0:T(8,128)(2,1)}, u32[]{:S(2)}, u32[]{:S(2)}) %collective-permute-start.5) | collective-permute-done | bytes 1638432 | tf_op jit(solution)/shard_map/ppermute | solution.py:125
  455.5 40.0 %collective-permute-done.12 = bf16[2,2,256,1024]{3,2,1,0:T(8,128)(2,1)S(1)} collective-permute-done((bf16[2,2,256,1024]{3,2,1,0:T(8,128)(2,1)}, bf16[2,2,256,1024]{3,2,1,0:T(8,128)(2,1)S(1)}, u32[]{:S(2)}, u32[]{:S(2)}) %collective-permute-start.12) | collective-permute-done | bytes 2097184 | tf_op jit(solution)/shard_map/ppermute | solution.py:125
  505.1 7.1 %collective-permute-done.9 = bf16[64,4096]{1,0:T(8,128)(2,1)S(1)} collective-permute-done((bf16[64,4096]{1,0:T(8,128)(2,1)}, bf16[64,4096]{1,0:T(8,128)(2,1)S(1)}, u32[]{:S(2)}, u32[]{:S(2)}) %collective-permute-start.9) | collective-permute-done | bytes 524320 | tf_op jit(solution)/shard_map/ppermute | solution.py:145
  517.7 29.1 %collective-permute-done.13 = bf16[2,256,1024]{2,1,0:T(8,128)(2,1)} collective-permute-done((bf16[2,256,1024]{2,1,0:T(8,128)(2,1)}, bf16[2,256,1024]{2,1,0:T(8,128)(2,1)}, u32[]{:S(2)}, u32[]{:S(2)}) %collective-permute-start.13) | collective-permute-done | bytes 1048608 | tf_op jit(solution)/shard_map/ppermute | solution.py:125
  552.0 16.1 %collective-permute-done.14 = bf16[256,1024]{1,0:T(8,128)(2,1)S(1)} collective-permute-done((bf16[256,1024]{1,0:T(8,128)(2,1)S(1)}, bf16[256,1024]{1,0:T(8,128)(2,1)S(1)}, u32[]{:S(2)}, u32[]{:S(2)}) %collective-permute-start.14) | collective-permute-done | bytes 524320 | tf_op jit(solution)/shard_map/ppermute | solution.py:125
  571.9 10.0 %reduce-scatter.5.cloned.1.call-done = bf16[64,1024]{1,0:T(8,128)(2,1)} async-done(((bf16[1024,1024]{1,0:T(8,128)(2,1)}), bf16[64,1024]{1,0:T(8,128)(2,1)}) %reduce-scatter.5.cloned.1.call-update) | async-done | bytes 131088 | tf_op jit(solution)/shard_map/reduce_scatter | solution.py:141
  (215 shorter events, 193.3 us)
Async XLA Ops:
  7.2 167.3 %all-gather.4.cloned.1.call-start = ((), (), s32[]{:S(2)}) async-start(), calls=%async_computation.6 | async-start | bytes 6963200 | tf_op jit(solution)/shard_map/all_gather | solution.py:189
  11.5 240.4 %all-gather.6.cloned.1.call-start = ((), (), s32[]{:S(2)}) async-start(), calls=%async_computation.7 | async-start | bytes 2228224 | tf_op jit(solution)/shard_map/all_gather | solution.py:192
  12.3 243.5 %all-gather.8.cloned.1.call-start = ((), (), s32[]{:S(2)}) async-start(), calls=%async_computation.8 | async-start | bytes 8912896 | tf_op jit(solution)/shard_map/all_gather | solution.py:193
  13.0 22.0 %collective-permute-start = (bf16[256,1024]{1,0:T(8,128)(2,1)}, bf16[256,1024]{1,0:T(8,128)(2,1)S(1)}, u32[]{:S(2)}, u32[]{:S(2)}) collective-permute-start(bf16[256,1024]{1,0:T(8,128)(2,1)} %param.32), channel_id=1, source_target_pairs={{0,4},{1,5},{2,6},{3,7},{4,0},{5,1},{6,2},{7,3},{8,12},{9,13},{10,... | collective-permute-start | bytes 1572872 | tf_op jit(solution)/shard_map/ppermute | solution.py:104
  36.3 78.0 %collective-permute-start.1 = (bf16[2,256,1024]{2,1,0:T(8,128)(2,1)S(1)}, bf16[2,256,1024]{2,1,0:T(8,128)(2,1)S(1)}, u32[]{:S(2)}, u32[]{:S(2)}) collective-permute-start(bf16[2,256,1024]{2,1,0:T(8,128)(2,1)S(1)} %pad_maximum_fusion.4), channel_id=1, source_target_pairs={{0,8},{1,9},{2,10},{3,11},{4,12},{5,13},{6,14},{7,15},{8,0},{9,1},... | collective-permute-start | bytes 3145736 | tf_op jit(solution)/shard_map/ppermute | solution.py:104
  115.5 53.6 %collective-permute-start.2 = (bf16[2,2,256,1024]{3,2,1,0:T(8,128)(2,1)S(1)}, bf16[2,2,256,1024]{3,2,1,0:T(8,128)(2,1)}, u32[]{:S(2)}, u32[]{:S(2)}) collective-permute-start(bf16[2,2,256,1024]{3,2,1,0:T(8,128)(2,1)S(1)} %pad_maximum_fusion.2), channel_id=1, source_target_pairs={{0,2},{1,3},{2,0},{3,1},{4,6},{5,7},{6,4},{7,5},{8,10},{9,11},{10,... | collective-permute-start | bytes 6291464 | tf_op jit(solution)/shard_map/ppermute | solution.py:104
  174.1 21.7 %collective-permute-start.3 = (bf16[2,2,2,256,1024]{4,3,2,1,0:T(8,128)(2,1)}, bf16[2,2,2,256,1024]{4,3,2,1,0:T(8,128)(2,1)}, u32[]{:S(2)}, u32[]{:S(2)}) collective-permute-start(bf16[2,2,2,256,1024]{4,3,2,1,0:T(8,128)(2,1)} %pad_maximum_fusion.1), channel_id=1, source_target_pairs={{0,1},{1,0},{2,3},{3,2},{4,5},{5,4},{6,7},{7,6},{8,9},{9,8},{10,11... | collective-permute-start | bytes 12582920 | tf_op jit(solution)/shard_map/ppermute | solution.py:104
  190.8 25.2 %all-to-all-start = ((bf16[256,3,2,512]{3,0,1,2:T(8,128)(2,1)}), bf16[256,3,2,512]{3,0,1,2:T(8,128)(2,1)}, u32[]{:S(2)}, u32[]{:S(2)}) async-start(bf16[256,3,2,512]{3,0,1,2:T(8,128)(2,1)} %copy.182), calls=%async_computation | async-start | bytes 3145728 | tf_op jit(solution)/shard_map/all_to_all | solution.py:228
  236.4 12.8 %all-to-all-start.1 = ((bf16[2,2,65536]{2,1,0:T(2,128)(2,1)}), bf16[2,2,65536]{2,1,0:T(2,128)(2,1)S(1)}, u32[]{:S(2)}, u32[]{:S(2)}) async-start(bf16[2,2,65536]{2,1,0:T(2,128)(2,1)} %reshape.258), calls=%async_computation.1 | async-start | bytes 1048576 | tf_op jit(solution)/shard_map/all_to_all | solution.py:240
  295.7 11.6 %all-to-all-start.2 = ((bf16[256,2,512]{2,0,1:T(8,128)(2,1)}), bf16[256,2,512]{2,0,1:T(8,128)(2,1)S(1)}, u32[]{:S(2)}, u32[]{:S(2)}) async-start(bf16[256,2,512]{2,0,1:T(8,128)(2,1)} %bitcast.195), calls=%async_computation.2 | async-start | bytes 1048576 | tf_op jit(solution)/shard_map/all_to_all | solution.py:288
  299.2 199.8 %reduce-scatter.3.cloned.1.call-start = ((), (), s32[]{:S(2)}) async-start(), calls=%async_computation.9 | async-start | bytes 8912896 | tf_op jit(solution)/shard_map/reduce_scatter | solution.py:141
  340.2 28.0 %all-to-all-start.3 = ((bf16[512,3,1,512]{3,1,2,0:T(4,128)(2,1)}), bf16[512,3,1,512]{3,1,2,0:T(4,128)(2,1)S(1)}, u32[]{:S(2)}, u32[]{:S(2)}) async-start(bf16[512,3,1,512]{3,1,2,0:T(4,128)(2,1)} %pad_maximum_fusion.3), calls=%async_computation.3 | async-start | bytes 4194304 | tf_op jit(solution)/shard_map/all_to_all | solution.py:302
  344.0 237.9 %reduce-scatter.5.cloned.1.call-start = ((), (), s32[]{:S(2)}) async-start(), calls=%async_computation.10 | async-start | bytes 2228224 | tf_op jit(solution)/shard_map/reduce_scatter | solution.py:141
  397.3 10.0 %collective-permute-start.4 = (bf16[2,2,2,64,3200]{4,3,1,0,2:T(8,128)(2,1)}, bf16[2,2,2,64,3200]{4,3,1,0,2:T(8,128)(2,1)}, u32[]{:S(2)}, u32[]{:S(2)}) collective-permute-start(bf16[2,2,2,64,3200]{4,3,1,0,2:T(8,128)(2,1)} %bitcast.194), channel_id=1, source_target_pairs={{0,1},{1,0},{2,3},{3,2},{4,5},{5,4},{6,7},{7,6},{8,9},{9,8},{10,11... | collective-permute-start | bytes 9830408 | tf_op jit(solution)/shard_map/ppermute | solution.py:125
  406.9 7.6 %collective-permute-start.11 = (bf16[2,2,2,256,1024]{4,3,1,0,2:T(8,128)(2,1)}, bf16[2,2,2,256,1024]{4,3,1,0,2:T(8,128)(2,1)}, u32[]{:S(2)}, u32[]{:S(2)}) collective-permute-start(bf16[2,2,2,256,1024]{4,3,1,0,2:T(8,128)(2,1)} %bitcast.193), channel_id=1, source_target_pairs={{0,1},{1,0},{2,3},{3,2},{4,5},{5,4},{6,7},{7,6},{8,9},{9,8},{10,11... | collective-permute-start | bytes 12582920 | tf_op jit(solution)/shard_map/ppermute | solution.py:125
  412.7 39.0 %collective-permute-start.5 = (bf16[2,2,64,3200]{3,2,1,0:T(8,128)(2,1)}, bf16[2,2,64,3200]{3,2,1,0:T(8,128)(2,1)}, u32[]{:S(2)}, u32[]{:S(2)}) collective-permute-start(bf16[2,2,64,3200]{3,2,1,0:T(8,128)(2,1)} %dynamic-slice_bitcast_fusion.1), channel_id=1, source_target_pairs={{0,2},{1,3},{2,0},{3,1},{4,6},{5,7},{6,4},{7,5},{8,10},{9,11},{10,... | collective-permute-start | bytes 4915208 | tf_op jit(solution)/shard_map/ppermute | solution.py:125
  422.3 73.3 %collective-permute-start.12 = (bf16[2,2,256,1024]{3,2,1,0:T(8,128)(2,1)}, bf16[2,2,256,1024]{3,2,1,0:T(8,128)(2,1)S(1)}, u32[]{:S(2)}, u32[]{:S(2)}) collective-permute-start(bf16[2,2,256,1024]{3,2,1,0:T(8,128)(2,1)} %dynamic-slice_bitcast_fusion), channel_id=1, source_target_pairs={{0,2},{1,3},{2,0},{3,1},{4,6},{5,7},{6,4},{7,5},{8,10},{9,11},{10,... | collective-permute-start | bytes 6291464 | tf_op jit(solution)/shard_map/ppermute | solution.py:125
  455.1 44.4 %collective-permute-start.6 = (bf16[2,64,3200]{2,1,0:T(8,128)(2,1)}, bf16[2,64,3200]{2,1,0:T(8,128)(2,1)}, u32[]{:S(2)}, u32[]{:S(2)}) collective-permute-start(bf16[2,64,3200]{2,1,0:T(8,128)(2,1)} %dynamic-slice_bitcast_fusion.3), channel_id=1, source_target_pairs={{0,8},{1,9},{2,10},{3,11},{4,12},{5,13},{6,14},{7,15},{8,0},{9,1},... | collective-permute-start | bytes 2457608 | tf_op jit(solution)/shard_map/ppermute | solution.py:125
  499.0 47.7 %collective-permute-start.13 = (bf16[2,256,1024]{2,1,0:T(8,128)(2,1)}, bf16[2,256,1024]{2,1,0:T(8,128)(2,1)}, u32[]{:S(2)}, u32[]{:S(2)}) collective-permute-start(bf16[2,256,1024]{2,1,0:T(8,128)(2,1)} %dynamic-slice_bitcast_fusion.2), channel_id=1, source_target_pairs={{0,8},{1,9},{2,10},{3,11},{4,12},{5,13},{6,14},{7,15},{8,0},{9,1},... | collective-permute-start | bytes 3145736 | tf_op jit(solution)/shard_map/ppermute | solution.py:125
  499.0 13.2 %collective-permute-start.9 = (bf16[64,4096]{1,0:T(8,128)(2,1)}, bf16[64,4096]{1,0:T(8,128)(2,1)S(1)}, u32[]{:S(2)}, u32[]{:S(2)}) collective-permute-start(bf16[64,4096]{1,0:T(8,128)(2,1)} %reduce-scatter.3.cloned.1.call-done), channel_id=1, source_target_pairs={{0,16},{16,0},{1,17},{17,1},{2,18},{18,2},{3,19},{19,3},{4,20},{20... | collective-permute-start | bytes 1572872 | tf_op jit(solution)/shard_map/ppermute | solution.py:145
  501.9 46.9 %collective-permute-start.7 = (bf16[64,3200]{1,0:T(8,128)(2,1)}, bf16[64,3200]{1,0:T(8,128)(2,1)}, u32[]{:S(2)}, u32[]{:S(2)}) collective-permute-start(bf16[64,3200]{1,0:T(8,128)(2,1)} %dynamic-slice_bitcast_fusion.5), channel_id=1, source_target_pairs={{0,4},{1,5},{2,6},{3,7},{4,0},{5,1},{6,2},{7,3},{8,12},{9,13},{10,... | collective-permute-start | bytes 1228808 | tf_op jit(solution)/shard_map/ppermute | solution.py:125
  548.7 19.4 %collective-permute-start.14 = (bf16[256,1024]{1,0:T(8,128)(2,1)S(1)}, bf16[256,1024]{1,0:T(8,128)(2,1)S(1)}, u32[]{:S(2)}, u32[]{:S(2)}) collective-permute-start(bf16[256,1024]{1,0:T(8,128)(2,1)S(1)} %dynamic-slice_bitcast_fusion.4), channel_id=1, source_target_pairs={{0,4},{1,5},{2,6},{3,7},{4,0},{5,1},{6,2},{7,3},{8,12},{9,13},{10,... | collective-permute-start | bytes 1572872 | tf_op jit(solution)/shard_map/ppermute | solution.py:125
  549.9 19.3 %collective-permute-start.8 = (bf16[64,3200]{1,0:T(8,128)(2,1)S(1)}, bf16[64,3200]{1,0:T(8,128)(2,1)S(1)}, u32[]{:S(2)}, u32[]{:S(2)}) collective-permute-start(bf16[64,3200]{1,0:T(8,128)(2,1)S(1)} %fusion.30), channel_id=1, source_target_pairs={{0,16},{16,0},{1,17},{17,1},{2,18},{18,2},{3,19},{19,3},{4,20},{20... | collective-permute-start | bytes 1228808 | tf_op jit(solution)/shard_map/ppermute | solution.py:145
  568.3 15.0 %collective-permute-start.15 = (bf16[256,1024]{1,0:T(8,128)(2,1)S(1)}, bf16[256,1024]{1,0:T(8,128)(2,1)S(1)}, u32[]{:S(2)}, u32[]{:S(2)}) collective-permute-start(bf16[256,1024]{1,0:T(8,128)(2,1)S(1)} %fusion.24), channel_id=1, source_target_pairs={{0,16},{16,0},{1,17},{17,1},{2,18},{18,2},{3,19},{19,3},{4,20},{20... | collective-permute-start | bytes 1572872 | tf_op jit(solution)/shard_map/ppermute | solution.py:145
  (34 other events, 304.7 us)
Sparse Core Ops, SparseCore 0:
  11.6 103.8 all-gather.3
  117.7 46.2 all-gather.5
  166.2 73.8 all-gather.7
  303.8 105.1 reduce-scatter.2
  517.8 64.0 reduce-scatter.4
